TPU v7x, 512 devices: a whole 4x4x16 slice. The times are simulated.
512 devices in a mesh: gz: 64 (over z, x_lo, core), step: 8 (over y, x_hi).
Axes of the slice: x: 4 (x_hi: 2, x_lo: 2; x = x_hi * 2 + x_lo), y: 4, z: 16, core: 2. Of those that a mesh axis runs over, the one named last changes fastest.
Arguments:
- reference_volume: bfloat16 [512, 16, 32, 128], P('gz', None, 'step'), may hold values from -6 to 6
- deformed: bfloat16 [8, 512, 16, 32, 128], P('step', 'gz'), may hold values from -6 to 6
- centres: int32 [8, 64, 2], P('step', 'gz'), may hold values from 0 to 124
- tether: float32 [64, 2], P('gz'), may hold values from 0.2 to 200
Outputs:
- displacement: float32 [8, 64, 2, 3], P('step', 'gz')
All inputs are finite; a program needn't handle non-finite values.
Results may differ from a plain program's by a relative error of at most 0.0003.
Values may be sent and summed in bfloat16 or wider, within the bound.
No kernel may reach another device: no remote copies, remote signals or barrier semaphores. Data moves between devices by JAX's collectives and lax.ppermute only.
A program may use at most 128 MiB of HBM per device.

v0:
```python
import math

import jax
import jax.numpy as jnp
from jax import lax
from jax.sharding import PartitionSpec as P

SB = 16


def padded_2(x, sides, width):
    for axis, dim in sides:
        devices, length = (lax.axis_size(axis), x.shape[dim])
        up = [(i, (i + 1) % devices) for i in range(devices - 1)]
        down = [(j, i) for i, j in up]
        last = lax.slice_in_dim(x, length - width, length, axis=dim)
        leading = lax.slice_in_dim(x, 0, width, axis=dim)
        before = lax.ppermute(last, axis, up)
        after = lax.ppermute(leading, axis, down)
        x = jnp.concatenate([before, x, after], axis=dim)
    return x


def prefix(x, axis, combine, identity):
    devices, position = (lax.axis_size(axis), lax.axis_index(axis))
    everything = jax.tree.map(lambda part: lax.all_gather(part, axis), x)
    start = jax.tree.map(
        lambda part, zero: jnp.broadcast_to(jnp.asarray(zero, part.dtype), part.shape), x, identity
    )

    def step(k, before):
        reached = k < position
        new = combine(before, jax.tree.map(lambda part: part[k], everything))
        return jax.tree.map(lambda a, b: jnp.where(reached, a, b), new, before)

    return lax.fori_loop(0, devices, step, start)


def peak_fit(scores, code_idx, tether):
    cube = scores.reshape(scores.shape[:-1] + (3, 3, 3))
    profiles = [cube.sum(axis=(-2, -1)), cube.sum(axis=(-3, -1)), cube.sum(axis=(-3, -2))]
    offsets = [code_idx // 25 - 2, code_idx // 5 % 5 - 2, code_idx % 5 - 2]
    moves = []
    bends = []
    for profile, offset in zip(profiles, offsets):
        lower = profile[..., 0]
        middle = profile[..., 1]
        upper = profile[..., 2]
        bend = jnp.maximum(2.0 * middle - lower - upper, 1.0)
        delta = jnp.clip((upper - lower) / (2.0 * bend), -1.0, 1.0)
        moves.append(offset.astype(jnp.float32) + delta)
        bends.append(bend)
    measured = jnp.stack(moves, axis=-1)
    quality = (bends[0] + bends[1] + bends[2]) / 3.0
    gain = quality / (quality + tether)
    return (measured, gain)


def shards(reference_volume, deformed, centres, tether):
    volume_now = deformed[0]
    planes, channels, rows_all, width_x = volume_now.shape
    block_count = centres.shape[2]
    padded = padded_2(volume_now, (("gz", 0),), 3)
    padded = jnp.pad(padded, ((0, 0), (0, 0), (3, 3), (3, 3)))
    code_idx = centres[0, 0]
    shift_z = code_idx // 25 - 2
    shift_y = code_idx // 5 % 5 - 2
    shift_x = code_idx % 5 - 2
    blocks = jnp.arange(block_count, dtype=jnp.int32)
    windows = []
    for block in range(block_count):
        windows.append(
            lax.dynamic_slice(
                padded,
                (
                    2 + shift_z[block],
                    jnp.int32(0),
                    block * SB + 2 + shift_y[block],
                    2 + shift_x[block],
                ),
                (planes + 2, channels, SB + 2, width_x + 2),
            )
        )
    aligned = [
        jnp.concatenate([window[:, :, along_y : along_y + SB] for window in windows], axis=2)
        for along_y in range(3)
    ]
    whole_ref = lax.all_gather(reference_volume, "step", axis=2, tiled=True)
    count = whole_ref.shape[2]
    global_rows = jnp.arange(count, dtype=jnp.int32)
    member_float = ((global_rows // SB)[:, None] == blocks[None, :]).astype(jnp.float32)
    values = [None] * 27
    for along_y in range(3):
        rows_moved = aligned[along_y]
        for along_z in range(3):
            for along_x in range(3):
                moved = rows_moved[along_z : along_z + planes, :, :, along_x : along_x + width_x]
                values[along_z * 9 + along_y * 3 + along_x] = jnp.einsum(
                    "zcrx,zcrx->r", whole_ref, moved, preferred_element_type=jnp.float32
                )
    row_scores = jnp.stack(values, axis=1)
    totals = jnp.dot(
        member_float.T,
        row_scores,
        precision=lax.Precision.HIGHEST,
        preferred_element_type=jnp.float32,
    )
    scores = totals * (1.0 / math.sqrt(planes * channels * SB * width_x))
    measured, gain = peak_fit(scores, code_idx, tether[0])
    rimmed = padded_2(measured[None], (("gz", 0),), 1)
    zsum = rimmed[0] + 2.0 * rimmed[1] + rimmed[2]
    ypad = jnp.pad(zsum, ((1, 1), (0, 0)))
    ysum = ypad[:-2] + 2.0 * ypad[1:-1] + ypad[2:]
    position = lax.axis_index("gz")
    slab_count = lax.axis_size("gz")
    weight_z = (
        2.0 + (position > 0).astype(jnp.float32) + (position < slab_count - 1).astype(jnp.float32)
    )
    weight_y = (
        2.0 + (blocks > 0).astype(jnp.float32) + (blocks < block_count - 1).astype(jnp.float32)
    )
    smooth = ysum / (weight_z * weight_y)[:, None]
    keep = 1.0 - gain
    drive = gain[:, None] * smooth

    def compose(earlier, later):
        return (earlier[0] * later[0], later[0][:, None] * earlier[1] + later[1])

    identity = (jnp.ones((block_count,), jnp.float32), jnp.zeros((block_count, 3), jnp.float32))
    prior_keep, prior_drive = prefix((keep, drive), "step", compose, identity)
    result = keep[:, None] * prior_drive + drive
    return result[None, None]


def solution(mesh):
    placed = (
        P("gz", None, "step", None),
        P("step", "gz", None, None, None),
        P("step", "gz", None),
        P("gz", None),
    )
    return jax.shard_map(
        shards, mesh=mesh, in_specs=placed, out_specs=P("step", "gz", None, None), check_vma=False
    )
```

profile of v0, /device:TPU:6, one launch (start us, length us, event | category | flops | bytes accessed | tf_op | source)
XLA Modules:
  0.0 186.3 jit_solution(5447940835540376289)
XLA Ops:
  6.5 1.3 slice_bitcast_fusion.1
  7.8 1.9 %collective-permute-start = (bf16[3,16,32,128]{3,2,1,0:T(8,128)(2,1)S(1)}, bf16[3,16,32,128]{3,2,1,0:T(8,128)(2,1)S(1)}, u32[]{:S(2)}, u32[]{:S(2)}) collective-permute-start(bf16[3,16,32,128]{3,2,1,0:T(8,128)(2,1)S(1)} %get-tuple-element.221), channel_id=1, source_target_pairs={{0,8},{8,16},{16,24},{24,32},{32,40},{40,48},{48,56},{56,64},{64,7... | collective-permute-start | bytes 1179656 | tf_op jit(solution)/shard_map/ppermute | solution.py:18
  9.7 3.6 %collective-permute-start.1 = (bf16[3,16,32,128]{3,2,1,0:T(8,128)(2,1)S(1)}, bf16[3,16,32,128]{3,2,1,0:T(8,128)(2,1)S(1)}, u32[]{:S(2)}, u32[]{:S(2)}) collective-permute-start(bf16[3,16,32,128]{3,2,1,0:T(8,128)(2,1)S(1)} %get-tuple-element.222), channel_id=1, source_target_pairs={{8,0},{16,8},{24,16},{32,24},{40,32},{48,40},{56,48},{64,56},{72,6... | collective-permute-start | bytes 1179656 | tf_op jit(solution)/shard_map/ppermute | solution.py:19
  13.4 1.6 copy.36
  15.0 0.7 fusion.126
  15.6 0.6 fusion.137
  21.3 0.6 fusion.139
  24.3 0.7 compare_bitcast_fusion
  25.6 4.0 %select_maximum_fusion = bf16[14,16,38,134]{3,2,1,0:T(8,128)(2,1)S(1)} fusion(bf16[3,16,32,128]{3,2,1,0:T(8,128)(2,1)S(1)} %collective-permute-done.1, bf16[8,16,32,128]{3,2,1,0:T(8,128)(2,1)S(1)} %bitcast.273, bf16[3,16,32,128]{3,2,1,0:T(8,128)(2,1)S(1)} %collective-permute-done), kind=kLoop, calls=%fused_computation.85 | loop fusion | flops 21671552 | bytes 4116224 | tf_op jit(solution)/shard_map/concatenate | solution.py:20
  29.6 7.2 %constant_dynamic-slice_fusion.2 = (bf16[10,16,16,130]{3,2,1,0:T(8,128)(2,1)S(1)}, bf16[10,16,16,130]{3,2,1,0:T(8,128)(2,1)S(1)}, bf16[10,16,16,130]{3,2,1,0:T(8...) fusion(bf16[14,16,38,134]{3,2,1,0:T(8,128)(2,1)S(1)} %select_ma, ...), kind=kLoop, calls=%fused_computation.222 | loop fusion | bytes 7987240 | tf_op jit(solution)/shard_map/slice | solution.py:85
  36.8 11.3 %fusion.96 = (f32[32,16,128,8]{2,0,1,3:T(8,128)S(1)}, f32[32,16,128,8]{2,0,1,3:T(8,128)}, f32[32,16,128,8]{2,0,1,3:T(8,128)}, f32[32,16,128,8]{2,0,1,3:T(8,128)}...) fusion(bf16[10,16,16,130]{3,2,1,0:T(8,128)(2,1)} %get-tuple-ele, ...), kind=kLoop, calls=%fused_computation.180 | loop fusion | flops 23592960 | bytes 20205568
  48.1 7.9 %fusion.72 = (f32[32,16,128,8]{2,0,1,3:T(8,128)}, f32[32,16,128,8]{2,0,1,3:T(8,128)}, f32[32,16,128,8]{2,0,1,3:T(8,128)}, f32[32,16,128,8]{2,0,1,3:T(8,128)}, f3...) fusion(bf16[10,16,16,130]{3,2,1,0:T(8,128)(2,1)S(1)} %get-tuple, ...), kind=kLoop, calls=%fused_computation.156 | loop fusion | flops 23592960 | bytes 20205568
  55.9 7.9 %fusion.48 = (f32[32,16,128,8]{2,0,1,3:T(8,128)}, f32[32,16,128,8]{2,0,1,3:T(8,128)}, f32[32,16,128,8]{2,0,1,3:T(8,128)}, f32[32,16,128,8]{2,0,1,3:T(8,128)}, f3...) fusion(bf16[10,16,16,130]{3,2,1,0:T(8,128)(2,1)S(1)} %get-tuple, ...), kind=kLoop, calls=%fused_computation.132 | loop fusion | flops 23592960 | bytes 20205568
  63.8 18.0 %all-gather.5.cloned.1.call-done = bf16[8,16,32,128]{3,1,0,2:T(8,128)(2,1)} async-done(((bf16[8,16,4,128]{3,1,0,2:T(8,128)(2,1)}), bf16[8,16,32,128]{3,1,0,2:T(8,128)(2,1)}) %all-gather.5.cloned.1.call-update) | async-done | bytes 1048592 | tf_op jit(solution)/shard_map/all_gather | solution.py:88
  81.8 14.9 %fusion.15 = (f32[32]{0:T(128)S(1)}, f32[32]{0:T(128)S(1)}, f32[32]{0:T(128)S(1)}, f32[32]{0:T(128)S(1)}, f32[32]{0:T(128)S(1)}, /*index=5*/f32[32]{0:T(128)S(1)}, f32[32]{0:T(128)S(1)}, f32[32]{0:T(128)S(1)}, f32[32]{0:T(128)S(1)}) fusion(f32[32,16,128,8]{2,0,1,3:T(8,128)} %get-tuple-element.215, bf16[8,16,32,128]{3,1,0,2:T(8,128)(2,1)} %all-gather.5.cloned.1.call-done, ...), kind=kLoop, calls=%fused_computation.98 | loop fusion | flops 9961184 | bytes 19924096 | tf_op jit(solution)/shard_map/zcrx,zcrx->r/dot_general | solution.py:98
  96.8 33.0 %fusion.33 = (f32[32]{0:T(128)S(1)}, f32[32]{0:T(128)S(1)}, f32[32]{0:T(128)S(1)}, f32[32]{0:T(128)S(1)}, f32[32]{0:T(128)S(1)}, /*index=5*/f32[32]{0:T(128)S(1)...) fusion(f32[32,16,128,8]{2,0,1,3:T(8,128)} %get-tuple-element.21, ...), kind=kLoop, calls=%fused_computation.116 | loop fusion | flops 19398080 | bytes 38799616 | tf_op jit(solution)/shard_map/zcrx,zcrx->r/dot_general | solution.py:98
  129.9 0.2 convolution_multiply_fusion
  130.4 0.2 fusion.134
  130.7 1.9 %collective-permute-start.2 = (f32[1,2,3]{2,1,0:T(2,128)S(1)}, f32[1,2,3]{2,1,0:T(2,128)S(1)}, u32[]{:S(2)}, u32[]{:S(2)}) collective-permute-start(f32[1,2,3]{2,1,0:T(2,128)S(1)} %fusion.135), channel_id=1, source_target_pairs={{0,8},{8,16},{16,24},{24,32},{32,40},{40,48},{48,56},{56,64},{64,7... | collective-permute-start | bytes 80 | tf_op jit(solution)/shard_map/ppermute | solution.py:18
  132.6 3.6 %collective-permute-start.3 = (f32[1,2,3]{2,1,0:T(2,128)S(1)}, f32[1,2,3]{2,1,0:T(2,128)S(1)}, u32[]{:S(2)}, u32[]{:S(2)}) collective-permute-start(f32[1,2,3]{2,1,0:T(2,128)S(1)} %fusion.135), channel_id=1, source_target_pairs={{8,0},{16,8},{24,16},{32,24},{40,32},{48,40},{56,48},{64,56},{72,6... | collective-permute-start | bytes 80 | tf_op jit(solution)/shard_map/ppermute | solution.py:19
  136.4 20.1 %all-gather.1 = f32[8,1,2]{2,1,0:T(1,128)S(1)} all-gather(f32[1,1,2]{2,1,0:T(1,128)S(1)} %subtract_bitcast_fusion), channel_id=1, replica_groups=mesh['gz'=64,'step'=8] {'step'}, dimensions={0}, use_global_device_ids=true | all-gather | bytes 72 | tf_op jit(solution)/shard_map/all_gather | solution.py:26
  156.7 21.4 %all-gather.2 = f32[8,2,3]{2,1,0:T(2,128)S(1)} all-gather(f32[1,2,3]{2,1,0:T(2,128)S(1)} %fusion.141), channel_id=2, replica_groups=mesh['gz'=64,'step'=8] {'step'}, dimensions={0}, use_global_device_ids=true | all-gather | bytes 216 | tf_op jit(solution)/shard_map/all_gather | solution.py:26
  178.1 0.7 while.14
  178.8 0.6 add_bitcast_fusion
  (61 shorter events, 2.2 us)
Async XLA Ops:
  6.5 19.1 %copy-start.7 = (bf16[1,8,16,32,128]{4,3,2,1,0:T(8,128)(2,1)S(1)}, bf16[1,8,16,32,128]{4,3,2,1,0:T(8,128)(2,1)}, u32[]{:S(2)}) copy-start(bf16[1,8,16,32,128]{4,3,2,1,0:T(8,128)(2,1)} %param.7) | copy-start | bytes 3145732
  6.5 18.8 %copy-start.8 = (s32[1,1,2]{2,1,0:T(1,128)S(1)}, s32[1,1,2]{2,1,0:T(1,128)}, u32[]{:S(2)}) copy-start(s32[1,1,2]{2,1,0:T(1,128)} %param.8) | copy-start | bytes 28
  6.5 18.9 %copy-start.9 = (f32[1,2]{1,0:T(1,128)S(1)}, f32[1,2]{1,0:T(1,128)}, u32[]{:S(2)}) copy-start(f32[1,2]{1,0:T(1,128)} %param.9) | copy-start | bytes 28
  6.5 75.2 %all-gather.5.cloned.1.call-start = ((), (), s32[]{:S(2)}) async-start(), calls=%async_computation | async-start | bytes 1179648 | tf_op jit(solution)/shard_map/all_gather | solution.py:88
  7.8 17.8 %collective-permute-start = (bf16[3,16,32,128]{3,2,1,0:T(8,128)(2,1)S(1)}, bf16[3,16,32,128]{3,2,1,0:T(8,128)(2,1)S(1)}, u32[]{:S(2)}, u32[]{:S(2)}) collective-permute-start(bf16[3,16,32,128]{3,2,1,0:T(8,128)(2,1)S(1)} %get-tuple-element.221), channel_id=1, source_target_pairs={{0,8},{8,16},{16,24},{24,32},{32,40},{40,48},{48,56},{56,64},{64,7... | collective-permute-start | bytes 1179656 | tf_op jit(solution)/shard_map/ppermute | solution.py:18
  9.7 15.9 %collective-permute-start.1 = (bf16[3,16,32,128]{3,2,1,0:T(8,128)(2,1)S(1)}, bf16[3,16,32,128]{3,2,1,0:T(8,128)(2,1)S(1)}, u32[]{:S(2)}, u32[]{:S(2)}) collective-permute-start(bf16[3,16,32,128]{3,2,1,0:T(8,128)(2,1)S(1)} %get-tuple-element.222), channel_id=1, source_target_pairs={{8,0},{16,8},{24,16},{32,24},{40,32},{48,40},{56,48},{64,56},{72,6... | collective-permute-start | bytes 1179656 | tf_op jit(solution)/shard_map/ppermute | solution.py:19
  81.8 15.0 %copy-start = (f32[32,16,128,8]{2,0,1,3:T(8,128)S(1)}, f32[32,16,128,8]{2,0,1,3:T(8,128)}, u32[]{:S(2)}) copy-start(f32[32,16,128,8]{2,0,1,3:T(8,128)} %get-tuple-element.198) | copy-start | bytes 6291460
  81.8 15.0 %copy-start.1 = (f32[32,16,128,8]{2,0,1,3:T(8,128)S(1)}, f32[32,16,128,8]{2,0,1,3:T(8,128)}, u32[]{:S(2)}) copy-start(f32[32,16,128,8]{2,0,1,3:T(8,128)} %get-tuple-element.199) | copy-start | bytes 6291460
  81.8 15.0 %copy-start.2 = (f32[32,16,128,8]{2,0,1,3:T(8,128)S(1)}, f32[32,16,128,8]{2,0,1,3:T(8,128)}, u32[]{:S(2)}) copy-start(f32[32,16,128,8]{2,0,1,3:T(8,128)} %get-tuple-element.200) | copy-start | bytes 6291460
  81.8 15.0 %copy-start.3 = (f32[32,16,128,8]{2,0,1,3:T(8,128)S(1)}, f32[32,16,128,8]{2,0,1,3:T(8,128)}, u32[]{:S(2)}) copy-start(f32[32,16,128,8]{2,0,1,3:T(8,128)} %get-tuple-element.201) | copy-start | bytes 6291460
  81.8 15.0 %copy-start.4 = (f32[32,16,128,8]{2,0,1,3:T(8,128)S(1)}, f32[32,16,128,8]{2,0,1,3:T(8,128)}, u32[]{:S(2)}) copy-start(f32[32,16,128,8]{2,0,1,3:T(8,128)} %get-tuple-element.202) | copy-start | bytes 6291460
  81.8 15.0 %copy-start.5 = (f32[32,16,128,8]{2,0,1,3:T(8,128)S(1)}, f32[32,16,128,8]{2,0,1,3:T(8,128)}, u32[]{:S(2)}) copy-start(f32[32,16,128,8]{2,0,1,3:T(8,128)} %get-tuple-element.203) | copy-start | bytes 6291460
  81.8 15.0 %copy-start.6 = (bf16[8,16,32,128]{3,1,0,2:T(8,128)(2,1)S(1)}, bf16[8,16,32,128]{3,1,0,2:T(8,128)(2,1)}, u32[]{:S(2)}) copy-start(bf16[8,16,32,128]{3,1,0,2:T(8,128)(2,1)} %all-gather.5.cloned.1.call-done) | copy-start | bytes 3145732
  130.7 25.8 %collective-permute-start.2 = (f32[1,2,3]{2,1,0:T(2,128)S(1)}, f32[1,2,3]{2,1,0:T(2,128)S(1)}, u32[]{:S(2)}, u32[]{:S(2)}) collective-permute-start(f32[1,2,3]{2,1,0:T(2,128)S(1)} %fusion.135), channel_id=1, source_target_pairs={{0,8},{8,16},{16,24},{24,32},{32,40},{40,48},{48,56},{56,64},{64,7... | collective-permute-start | bytes 80 | tf_op jit(solution)/shard_map/ppermute | solution.py:18
  132.6 23.9 %collective-permute-start.3 = (f32[1,2,3]{2,1,0:T(2,128)S(1)}, f32[1,2,3]{2,1,0:T(2,128)S(1)}, u32[]{:S(2)}, u32[]{:S(2)}) collective-permute-start(f32[1,2,3]{2,1,0:T(2,128)S(1)} %fusion.135), channel_id=1, source_target_pairs={{8,0},{16,8},{24,16},{32,24},{40,32},{48,40},{56,48},{64,56},{72,6... | collective-permute-start | bytes 80 | tf_op jit(solution)/shard_map/ppermute | solution.py:19
Sparse Core Ops, SparseCore 0:
  15.1 66.6 all-gather.4
where the time goes:
time: 187 us; the launch traced here: 186 us
  other arithmetic  82.3 us (44%)
  blocking collectives  41.5 us (22%)
  between operations  21 us (11%)
  waiting for transfers between devices  18 us (10%)
  local copies, waits for them, and re-layouts  12 us (6%)
  starting transfers between devices  11.1 us (6%)
    dot_general x2, other arithmetic, shards(): jnp.einsum('zcrx,zcrx->r', whole_ref, moved, preferred_element_type=jnp.f...  47.9 us
    all_gather x2, blocking collectives, prefix(): everything = jax.tree.map(lambda part: lax.all_gather(part, axis), x)  41.5 us
    unnamed x6, other arithmetic  27.1 us
    all_gather x1, waiting for transfers between devices, shards(): whole_ref = lax.all_gather(reference_volume, 'step', axis=2, tiled=True)  18 us
    ppermute x2, starting transfers between devices, padded_2(): after = lax.ppermute(leading, axis, down)  7.28 us
    slice x1, local copies, waits for them, and re-layouts, shards(): window[:, :, along_y:along_y + SB]  7.18 us
    concatenate x1, other arithmetic, padded_2(): x = jnp.concatenate([before, x, after], axis=dim)  3.97 us
    ppermute x2, starting transfers between devices, padded_2(): before = lax.ppermute(last, axis, up)  3.84 us
  transfers between devices with their start and end apart: 5, of which 1 were waited for; matrix products, arithmetic and copies ran while one was open for 23% of the time, Pallas kernels for 0%

commit v1 on v0

v1 whole, which is shorter than its diff:
```python
import math

import jax
import jax.numpy as jnp
from jax import lax
from jax.experimental import pallas as pl
from jax.experimental.pallas import tpu as pltpu
from jax.sharding import PartitionSpec as P

SB = 16
HALO = 3
PAD = 8


def fit_kernel(
    planes, channels, rows, width,
    code_ref, tether_ref, parity_ref, r_ref, d_ref, inner_ref, outer_ref,
    own_out, edge_out, deep, left, right,
):
    depth = channels * SB
    window = planes + 2
    zeros = jnp.zeros((channels, PAD, width), jnp.float32)
    parity = parity_ref[0]
    inner_at = (1 - parity) * (planes + HALO)
    outer_at = parity * (planes + HALO)
    for z in range(planes + 2 * HALO):
        deep[z, :, 0:PAD, :] = zeros
        deep[z, :, PAD + rows : 2 * PAD + rows, :] = zeros
    for z in range(planes):
        deep[z + HALO, :, PAD : PAD + rows, :] = d_ref[z].astype(jnp.float32)
    for z in range(HALO):
        deep[inner_at + z, :, PAD : PAD + rows, :] = inner_ref[z].astype(jnp.float32)
        deep[outer_at + z, :, PAD : PAD + rows, :] = outer_ref[z].astype(jnp.float32)

    lane = lax.broadcasted_iota(jnp.int32, (1, width), 1)
    line = lax.broadcasted_iota(jnp.int32, (width, width), 0)
    column = lax.broadcasted_iota(jnp.int32, (width, width), 1)
    scale = 1.0 / math.sqrt(planes * depth * width)
    bend_row = jnp.ones((1, width), jnp.float32)
    slope_row = jnp.zeros((1, width), jnp.float32)
    centre_row = jnp.zeros((1, width), jnp.float32)
    quality_row = jnp.ones((1, width), jnp.float32)
    tether_row = jnp.ones((1, width), jnp.float32)
    empty = jnp.zeros((width, depth), jnp.bfloat16)
    for tz in range(3):
        for p in range(window):
            if p < tz or p >= tz + planes:
                left[tz * width : (tz + 1) * width, p * depth : (p + 1) * depth] = empty

    for block in range(rows // SB):
        code = code_ref[0, 0, block]
        shift_z = lax.div(code, 25) - 2
        shift_y = lax.rem(lax.div(code, 5), 5) - 2
        shift_x = lax.rem(code, 5) - 2
        for z in range(planes):
            plane = r_ref[z, :, block * SB : (block + 1) * SB, :].astype(jnp.float32)
            turned = plane.reshape(depth, width).T.astype(jnp.bfloat16)
            for tz in range(3):
                p = z + tz
                left[tz * width : (tz + 1) * width, p * depth : (p + 1) * depth] = turned
        first_plane = shift_z + (HALO - 1)
        first_row = shift_y + (PAD - 1 + block * SB)
        for p in range(window):
            for ty in range(3):
                part = deep[first_plane + p, :, pl.ds(first_row + ty, SB), :]
                right[p * depth : (p + 1) * depth, ty * width : (ty + 1) * width] = (
                    part.reshape(depth, width).astype(jnp.bfloat16)
                )
        gram = jnp.dot(left[...], right[...], preferred_element_type=jnp.float32)
        cut = [
            [
                gram[tz * width : (tz + 1) * width, ty * width : (ty + 1) * width]
                for ty in range(3)
            ]
            for tz in range(3)
        ]
        along_z = [cut[t][0] + cut[t][1] + cut[t][2] for t in range(3)]
        along_y = [cut[0][t] + cut[1][t] + cut[2][t] for t in range(3)]
        whole = along_z[0] + along_z[1] + along_z[2]
        far = column - line - shift_x
        band = jnp.abs(far) <= 1
        upper = jnp.where(far == 1, whole, 0.0)
        lower = jnp.where(far == -1, whole, 0.0)
        middle = jnp.where(far == 0, whole, 0.0)
        bends = [
            jnp.where(band, 2.0 * g[1] - g[0] - g[2], 0.0) for g in (along_z, along_y)
        ] + [2.0 * middle - lower - upper]
        slopes = [jnp.where(band, g[2] - g[0], 0.0) for g in (along_z, along_y)] + [upper - lower]

        def total(values):
            return jnp.sum(jnp.sum(values, axis=0, keepdims=True), axis=1, keepdims=True) * scale

        sums = [jnp.maximum(total(b), 1.0) for b in bends]
        quality = (sums[0] + sums[1] + sums[2]) / 3.0
        for axis, shift in enumerate((shift_z, shift_y, shift_x)):
            here = lane == block * 3 + axis
            bend_row = jnp.where(here, sums[axis], bend_row)
            slope_row = jnp.where(here, total(slopes[axis]), slope_row)
            centre_row = jnp.where(here, shift.astype(jnp.float32), centre_row)
            quality_row = jnp.where(here, quality, quality_row)
            tether_row = jnp.where(here, tether_ref[0, block], tether_row)

    measured = centre_row + jnp.clip(slope_row / (2.0 * bend_row), -1.0, 1.0)
    gain = quality_row / (quality_row + tether_row)
    other = jnp.where(lane < 3, pltpu.roll(measured, width - 3, 1), pltpu.roll(measured, 3, 1))
    used = lane < 6
    filtered = jnp.where(used, 2.0 * measured + other, 0.0)
    gain = jnp.where(used, gain, 0.0)
    own_out[...] = filtered + pltpu.roll(gain, 8, 1)
    edge_out[...] = pltpu.roll(filtered, 16, 1)


def track_kernel(width, place_ref, all_ref, out_ref):
    step = place_ref[0]
    slab = place_ref[1]
    slabs = place_ref[2]
    parity = lax.rem(slab, 2)
    steps = all_ref.shape[0] // 2
    lane = lax.broadcasted_iota(jnp.int32, (1, width), 1)
    weight_z = 2.0 + (slab > 0).astype(jnp.float32) + (slab < slabs - 1).astype(jnp.float32)
    weight = jnp.full((1, width), weight_z * 3.0, jnp.float32)
    state = jnp.zeros((1, width), jnp.float32)
    even = all_ref[0:steps, 0, :]
    odd = all_ref[steps : 2 * steps, 0, :]
    mine = jnp.where(parity == 0, even, odd)
    partner = jnp.where(parity == 0, odd, even)
    gain = pltpu.roll(mine, width - 8, 1)
    outer = pltpu.roll(mine, width - 16, 1)
    smooth = (outer + 2.0 * mine + partner) / weight
    keep = 1.0 - gain
    drive = gain * smooth
    for s in range(steps):
        new = keep[s : s + 1] * state + drive[s : s + 1]
        state = jnp.where(s <= step, new, state)
    state = jnp.where(lane < 6, state, 0.0)
    out_ref[0, 0, 0:1, :] = state[:, 0:3]
    out_ref[0, 0, 1:2, :] = pltpu.roll(state, width - 3, 1)[:, 0:3]


def shards(reference_volume, deformed, centres, tether):
    steps, slabs = lax.axis_size("step"), lax.axis_size("gz")
    slab, step = lax.axis_index("gz"), lax.axis_index("step")
    parity = slab % 2
    volume_now = deformed[0]
    planes, channels, rows, width = volume_now.shape

    copies = jnp.broadcast_to(reference_volume[None], (steps,) + reference_volume.shape)
    gathered = lax.all_to_all(copies, "step", split_axis=0, concat_axis=0, tiled=True)
    whole_ref = gathered.transpose(1, 2, 0, 3, 4).reshape(planes, channels, rows, width)

    inside = [(i, i ^ 1) for i in range(slabs)]
    outside = [(i, i + 1) for i in range(1, slabs - 1, 2)]
    outside = outside + [(j, i) for i, j in outside]
    far = planes - HALO
    to_inner = lax.dynamic_slice_in_dim(volume_now, (1 - parity) * far, HALO, 0)
    to_outer = lax.dynamic_slice_in_dim(volume_now, parity * far, HALO, 0)
    inner = lax.ppermute(to_inner, "gz", inside)
    outer = lax.ppermute(to_outer, "gz", outside)

    smem = pl.BlockSpec(memory_space=pltpu.SMEM)
    vmem = pl.BlockSpec(memory_space=pltpu.VMEM)
    depth = channels * SB
    window = planes + 2
    own, edge = pl.pallas_call(
        lambda *refs: fit_kernel(planes, channels, rows, width, *refs),
        out_shape=[jax.ShapeDtypeStruct((1, width), jnp.float32)] * 2,
        in_specs=[smem] * 3 + [vmem] * 4,
        out_specs=[vmem] * 2,
        scratch_shapes=[
            pltpu.VMEM((planes + 2 * HALO, channels, rows + 2 * PAD, width), jnp.float32),
            pltpu.VMEM((3 * width, window * depth), jnp.bfloat16),
            pltpu.VMEM((window * depth, 3 * width), jnp.bfloat16),
        ],
        compiler_params=pltpu.CompilerParams(vmem_limit_bytes=40 * 1024 * 1024),
        name="fit",
    )(centres, tether, parity[None], whole_ref, volume_now, inner, outer)

    edge = lax.ppermute(edge, "gz", outside)
    row = (own + edge)[None]
    group = 2 * steps
    groups = [[group * i + j for j in range(group)] for i in range(slabs // 2)]
    everyone = lax.all_to_all(
        jnp.broadcast_to(row, (group, 1, width)),
        ("gz", "step"), split_axis=0, concat_axis=0, tiled=True, axis_index_groups=groups,
    )
    place = jnp.stack([step, slab, jnp.int32(slabs)]).astype(jnp.int32)
    return pl.pallas_call(
        lambda *refs: track_kernel(width, *refs),
        out_shape=jax.ShapeDtypeStruct((1, 1, 2, 3), jnp.float32),
        in_specs=[smem, vmem],
        out_specs=vmem,
        name="track",
    )(place, everyone)


def solution(mesh):
    placed = (
        P("gz", None, "step", None),
        P("step", "gz", None, None, None),
        P("step", "gz", None),
        P("gz", None),
    )
    return jax.shard_map(
        shards, mesh=mesh, in_specs=placed, out_specs=P("step", "gz", None, None), check_vma=False
    )
```

time: 187 us -> 57.9 us (0.31)
  the two profiles are of different devices: /device:TPU:6 before, /device:TPU:128 now
where the time goes in v1:
time: 57.9 us; the launch traced here: 57.6 us
  waiting for transfers between devices  29.9 us (52%)
  starting transfers between devices  16.5 us (28%)
  local copies, waits for them, and re-layouts  5.48 us (9%)
  Pallas kernels  5.05 us (9%)
  other arithmetic  0.6 us (1%)
    all_to_all x1, waiting for transfers between devices, shards(): lax.all_to_all(copies, 'step', split_axis=0, concat_axis=0, tiled=True)  18 us
    all_to_all x1, starting transfers between devices, shards(): lax.all_to_all(copies, 'step', split_axis=0, concat_axis=0, tiled=True)  7.06 us
    all_to_all x1, waiting for transfers between devices, shards(): lax.all_to_all(jnp.broadcast_to(row, (group, 1, width)), ('gz', 'step'),...  6.89 us
    ppermute x1, waiting for transfers between devices, shards(): edge = lax.ppermute(edge, 'gz', outside)  5.04 us
    pallas_call x1, Pallas kernels, shards(): pl.pallas_call(lambda *refs: fit_kernel(planes, channels, rows, width, *r...  3.6 us
    all_to_all x1, starting transfers between devices, shards(): lax.all_to_all(jnp.broadcast_to(row, (group, 1, width)), ('gz', 'step'),...  3.43 us
    broadcast_in_dim x1, local copies, waits for them, and re-layouts, shards(): jnp.broadcast_to(reference_volume[None], (steps,) + reference_volume.shape)  2.39 us
    ppermute x1, starting transfers between devices, shards(): outer = lax.ppermute(to_outer, 'gz', outside)  2.15 us
  transfers between devices with their start and end apart: 5, of which 3 were waited for; matrix products, arithmetic and copies ran while one was open for 3% of the time, Pallas kernels for 0%

profile of v1, /device:TPU:128, one launch (start us, length us, event | category | flops | bytes accessed | tf_op | source)
XLA Modules:
  0.0 57.6 jit_solution(12457736040661377378)
XLA Ops:
  0.0 2.4 %broadcast_in_dim.18 = bf16[8,8,16,4,128]{4,3,2,1,0:T(4,128)(2,1)} broadcast(bf16[8,16,4,128]{3,2,1,0:T(4,128)(2,1)} %param.4), dimensions={1,2,3,4} | broadcast | bytes 1179648 | tf_op jit(solution)/shard_map/broadcast_in_dim | solution.py:147
  2.4 0.0 copy-start
  2.4 7.1 %all-to-all-start = ((bf16[8,8,16,4,128]{4,3,2,1,0:T(4,128)(2,1)}), bf16[8,8,16,4,128]{4,3,2,1,0:T(4,128)(2,1)S(1)}, u32[]{:S(2)}, u32[]{:S(2)}) async-start(bf16[8,8,16,4,128]{4,3,2,1,0:T(4,128)(2,1)} %broadcast_in_dim.18), calls=%async_computation | async-start | bytes 2097152 | tf_op jit(solution)/shard_map/all_to_all | solution.py:148
  9.5 0.0 copy-done
  9.5 0.8 %dynamic-slice_bitcast_fusion = (bf16[3,16,32,128]{3,2,1,0:T(8,128)(2,1)S(1)}, bf16[3,16,32,128]{3,2,1,0:T(8,128)(2,1)}) fusion(bf16[1,8,16,32,128]{4,3,2,1,0:T(8,128)(2,1)S(1)} %copy-done, s32[]{:T(128)S(6)} %select_n.15, s32[]{:T(128)S(6)} %select_n.14), kind=kLoop, calls=%fused_computation | loop fusion | bytes 1572872 | tf_op jit(solution)/shard_map/dynamic_slice | solution.py:156
  10.3 1.9 %collective-permute-start = (bf16[3,16,32,128]{3,2,1,0:T(8,128)(2,1)}, bf16[3,16,32,128]{3,2,1,0:T(8,128)(2,1)S(1)}, u32[]{:S(2)}, u32[]{:S(2)}) collective-permute-start(bf16[3,16,32,128]{3,2,1,0:T(8,128)(2,1)} %get-tuple-element.10), channel_id=1, source_target_pairs={{0,8},{8,0},{16,24},{24,16},{32,40},{40,32},{48,56},{56,48},{64,72... | collective-permute-start | bytes 1179656 | tf_op jit(solution)/shard_map/ppermute | solution.py:157
  12.2 2.1 %collective-permute-start.1 = (bf16[3,16,32,128]{3,2,1,0:T(8,128)(2,1)S(1)}, bf16[3,16,32,128]{3,2,1,0:T(8,128)(2,1)S(1)}, u32[]{:S(2)}, u32[]{:S(2)}) collective-permute-start(bf16[3,16,32,128]{3,2,1,0:T(8,128)(2,1)S(1)} %get-tuple-element.9), channel_id=1, source_target_pairs={{8,16},{24,32},{40,48},{56,64},{72,80},{88,96},{104,112},{120,128}... | collective-permute-start | bytes 1179656 | tf_op jit(solution)/shard_map/ppermute | solution.py:158
  14.4 18.0 %all-to-all-done = bf16[8,8,16,4,128]{4,3,2,1,0:T(4,128)(2,1)S(1)} async-done(((bf16[8,8,16,4,128]{4,3,2,1,0:T(4,128)(2,1)}), bf16[8,8,16,4,128]{4,3,2,1,0:T(4,128)(2,1)S(1)}, u32[]{:S(2)}, u32[]{:S(2)}) %all-to-all-start) | async-done | bytes 1048608 | tf_op jit(solution)/shard_map/all_to_all | solution.py:148
  32.3 0.4 copy.5
  32.7 0.0 collective-permute-done.refs_5_
  32.7 0.0 collective-permute-done.1.refs_6_
  32.8 0.0 copy-start.1
  32.8 0.0 copy-start.2
  32.8 0.6 %copy-done.1 = s32[1,1,2]{2,1,0:T(1,128)S(1)} copy-done((s32[1,1,2]{2,1,0:T(1,128)S(1)}, s32[1,1,2]{2,1,0:T(1,128)}, u32[]{:S(2)}) %copy-start.1) | copy-done | bytes 32
  33.4 0.0 copy-done.2
  33.4 3.6 %fit.1 = (f32[1,128]{1,0:T(1,128)S(1)}, f32[1,128]{1,0:T(1,128)S(1)}) custom-call(s32[1,1,2]{2,1,0:T(1,128)S(1)} %copy-done.1, f32[1,2]{1,0:T(1,128)S(1)} %copy-done.2, s32[1]{0:T(128)} %bitcast.2.refs_2_, bf16[8,16,32,128]{3,2,1,0:T(8,128)(2,1)S(1)} %bitcast.12, bf16[8,16,32,128]{3,2,1,0:T(8,128)(2,1)S(1)} %bitcast.13, ...), custom_call_target="tpu_custom_call" | custom-call | tf_op jit(solution)/shard_map/fit/pallas_call | solution.py:164
  37.0 1.9 %collective-permute-start.2 = (f32[1,128]{1,0:T(1,128)S(1)}, f32[1,128]{1,0:T(1,128)S(1)}, u32[]{:S(2)}, u32[]{:S(2)}) collective-permute-start(f32[1,128]{1,0:T(1,128)S(1)} %get-tuple-element.8), channel_id=1, source_target_pairs={{8,16},{24,32},{40,48},{56,64},{72,80},{88,96},{104,112},{120,128}... | collective-permute-start | bytes 1544 | tf_op jit(solution)/shard_map/ppermute | solution.py:178
  38.9 5.0 %collective-permute-done.2 = f32[1,128]{1,0:T(1,128)S(1)} collective-permute-done((f32[1,128]{1,0:T(1,128)S(1)}, f32[1,128]{1,0:T(1,128)S(1)}, u32[]{:S(2)}, u32[]{:S(2)}) %collective-permute-start.2) | collective-permute-done | bytes 544 | tf_op jit(solution)/shard_map/ppermute | solution.py:178
  44.0 0.6 %broadcast_in_dim.20 = f32[16,1,128]{2,1,0:T(1,128)} broadcast(f32[128]{0:T(128)S(1)} %add_bitcast_fusion), dimensions={2} | broadcast | bytes 8704 | tf_op jit(solution)/shard_map/broadcast_in_dim | solution.py:183
  44.6 3.4 %all-to-all-start.1 = ((f32[16,1,128]{2,1,0:T(1,128)}), f32[16,1,128]{2,1,0:T(1,128)S(1)}, u32[]{:S(2)}, u32[]{:S(2)}) async-start(f32[16,1,128]{2,1,0:T(1,128)} %broadcast_in_dim.20), calls=%async_computation.1 | async-start | bytes 16384 | tf_op jit(solution)/shard_map/all_to_all | solution.py:182
  48.0 0.6 %pad_add_fusion.refs_0_ = s32[3]{0:T(128)} fusion(s32[1]{0:T(128)} %constant.26.clone.1, s32[1]{0:T(128)} %bitcast.1, s32[1]{0:T(128)} %bitcast), kind=kLoop, calls=%fused_computation.2 | loop fusion | flops 6 | bytes 24 | tf_op jit(solution)/shard_map/stack | solution.py:186
  48.6 6.9 %all-to-all-done.1.refs_1_ = f32[16,1,128]{2,1,0:T(1,128)S(1)} async-done(((f32[16,1,128]{2,1,0:T(1,128)}), f32[16,1,128]{2,1,0:T(1,128)S(1)}, u32[]{:S(2)}, u32[]{:S(2)}) %all-to-all-start.1) | async-done | bytes 8224 | tf_op jit(solution)/shard_map/all_to_all | solution.py:182
  55.5 0.6 %copy-done.3 = f32[16,1,128]{2,1,0:T(1,128)} copy-done((f32[16,1,128]{2,1,0:T(1,128)}, f32[16,1,128]{2,1,0:T(1,128)S(1)}, u32[]{:S(2)}) %copy-start.3) | copy-done | bytes 8216
  56.1 1.4 %track.1 = f32[1,1,2,3]{3,2,1,0:T(2,128)} custom-call(s32[3]{0:T(128)} %pad_add_fusion.refs_0_, f32[16,1,128]{2,1,0:T(1,128)} %copy-done.3), custom_call_target="tpu_custom_call" | custom-call | tf_op jit(solution)/shard_map/track/pallas_call | solution.py:187
  (2 shorter events, 0.0 us)
Async XLA Ops:
  2.4 7.1 %copy-start = (bf16[1,8,16,32,128]{4,3,2,1,0:T(8,128)(2,1)S(1)}, bf16[1,8,16,32,128]{4,3,2,1,0:T(8,128)(2,1)}, u32[]{:S(2)}) copy-start(bf16[1,8,16,32,128]{4,3,2,1,0:T(8,128)(2,1)} %param.5) | copy-start | bytes 3145732
  2.4 29.9 %all-to-all-start = ((bf16[8,8,16,4,128]{4,3,2,1,0:T(4,128)(2,1)}), bf16[8,8,16,4,128]{4,3,2,1,0:T(4,128)(2,1)S(1)}, u32[]{:S(2)}, u32[]{:S(2)}) async-start(bf16[8,8,16,4,128]{4,3,2,1,0:T(4,128)(2,1)} %broadcast_in_dim.18), calls=%async_computation | async-start | bytes 2097152 | tf_op jit(solution)/shard_map/all_to_all | solution.py:148
  10.3 22.4 %collective-permute-start = (bf16[3,16,32,128]{3,2,1,0:T(8,128)(2,1)}, bf16[3,16,32,128]{3,2,1,0:T(8,128)(2,1)S(1)}, u32[]{:S(2)}, u32[]{:S(2)}) collective-permute-start(bf16[3,16,32,128]{3,2,1,0:T(8,128)(2,1)} %get-tuple-element.10), channel_id=1, source_target_pairs={{0,8},{8,0},{16,24},{24,16},{32,40},{40,32},{48,56},{56,48},{64,72... | collective-permute-start | bytes 1179656 | tf_op jit(solution)/shard_map/ppermute | solution.py:157
  12.2 20.5 %collective-permute-start.1 = (bf16[3,16,32,128]{3,2,1,0:T(8,128)(2,1)S(1)}, bf16[3,16,32,128]{3,2,1,0:T(8,128)(2,1)S(1)}, u32[]{:S(2)}, u32[]{:S(2)}) collective-permute-start(bf16[3,16,32,128]{3,2,1,0:T(8,128)(2,1)S(1)} %get-tuple-element.9), channel_id=1, source_target_pairs={{8,16},{24,32},{40,48},{56,64},{72,80},{88,96},{104,112},{120,128}... | collective-permute-start | bytes 1179656 | tf_op jit(solution)/shard_map/ppermute | solution.py:158
  32.8 0.7 %copy-start.1 = (s32[1,1,2]{2,1,0:T(1,128)S(1)}, s32[1,1,2]{2,1,0:T(1,128)}, u32[]{:S(2)}) copy-start(s32[1,1,2]{2,1,0:T(1,128)} %refs_0_.1) | copy-start | bytes 28
  32.8 0.7 %copy-start.2 = (f32[1,2]{1,0:T(1,128)S(1)}, f32[1,2]{1,0:T(1,128)}, u32[]{:S(2)}) copy-start(f32[1,2]{1,0:T(1,128)} %refs_1_.1) | copy-start | bytes 28
  37.0 7.0 %collective-permute-start.2 = (f32[1,128]{1,0:T(1,128)S(1)}, f32[1,128]{1,0:T(1,128)S(1)}, u32[]{:S(2)}, u32[]{:S(2)}) collective-permute-start(f32[1,128]{1,0:T(1,128)S(1)} %get-tuple-element.8), channel_id=1, source_target_pairs={{8,16},{24,32},{40,48},{56,64},{72,80},{88,96},{104,112},{120,128}... | collective-permute-start | bytes 1544 | tf_op jit(solution)/shard_map/ppermute | solution.py:178
  44.6 10.9 %all-to-all-start.1 = ((f32[16,1,128]{2,1,0:T(1,128)}), f32[16,1,128]{2,1,0:T(1,128)S(1)}, u32[]{:S(2)}, u32[]{:S(2)}) async-start(f32[16,1,128]{2,1,0:T(1,128)} %broadcast_in_dim.20), calls=%async_computation.1 | async-start | bytes 16384 | tf_op jit(solution)/shard_map/all_to_all | solution.py:182
  55.5 0.6 %copy-start.3 = (f32[16,1,128]{2,1,0:T(1,128)}, f32[16,1,128]{2,1,0:T(1,128)S(1)}, u32[]{:S(2)}) copy-start(f32[16,1,128]{2,1,0:T(1,128)S(1)} %all-to-all-done.1.refs_1_) | copy-start | bytes 24580

commit v2 on v1

v2 whole, which is shorter than its diff:
```python
import math

import jax
import jax.numpy as jnp
from jax import lax
from jax.experimental import pallas as pl
from jax.experimental.pallas import tpu as pltpu
from jax.sharding import PartitionSpec as P

SB = 16
HALO = 3
PAD = 8
MIB = 1024 * 1024


def offsets(code):
    return (
        lax.div(code, 25) - 2,
        lax.rem(lax.div(code, 5), 5) - 2,
        lax.rem(code, 5) - 2,
    )


def fit_kernel(
    settings_hbm, r_ref, d_ref, inner_ref, outer_ref,
    own_out, edge_out, deep, left, right, settings, arrived
):
    planes, channels, rows, width = r_ref.shape
    depth = channels * SB
    window = planes + 2
    fetch = pltpu.make_async_copy(settings_hbm, settings, arrived)
    fetch.start()
    lane = lax.broadcasted_iota(jnp.int32, (1, width), 1)
    line = lax.broadcasted_iota(jnp.int32, (width, width), 0)
    column = lax.broadcasted_iota(jnp.int32, (width, width), 1)
    scale = 1.0 / math.sqrt(planes * depth * width)
    bend_row = jnp.ones((1, width), jnp.float32)
    slope_row = jnp.zeros((1, width), jnp.float32)
    centre_row = jnp.zeros((1, width), jnp.float32)
    quality_row = jnp.ones((1, width), jnp.float32)
    tether_row = jnp.ones((1, width), jnp.float32)
    empty = jnp.zeros((width, depth), jnp.bfloat16)
    for tz in range(3):
        for p in range(window):
            if p < tz or p >= tz + planes:
                left[tz * width : (tz + 1) * width, p * depth : (p + 1) * depth] = empty
    zeros = jnp.zeros((channels, PAD, width), jnp.float32)
    fetch.wait()
    parity = lax.rem(lax.axis_index("gz"), 2)
    inner_at = (1 - parity) * (planes + HALO)
    outer_at = parity * (planes + HALO)
    for z in range(planes + 2 * HALO):
        deep[z, :, 0:PAD, :] = zeros
        deep[z, :, PAD + rows : 2 * PAD + rows, :] = zeros
    for z in range(HALO):
        deep[inner_at + z, :, PAD : PAD + rows, :] = inner_ref[z].astype(jnp.float32)
        deep[outer_at + z, :, PAD : PAD + rows, :] = outer_ref[z].astype(jnp.float32)
    for z in range(planes):
        deep[z + HALO, :, PAD : PAD + rows, :] = d_ref[z].astype(jnp.float32)

    for block in range(rows // SB):
        shifts = offsets(settings[0, block].astype(jnp.int32))
        for z in range(planes):
            plane = r_ref[z, :, block * SB : (block + 1) * SB, :].astype(jnp.float32)
            turned = plane.reshape(depth, width).T.astype(jnp.bfloat16)
            for tz in range(3):
                p = z + tz
                left[tz * width : (tz + 1) * width, p * depth : (p + 1) * depth] = turned
        first_plane = shifts[0] + (HALO - 1)
        first_row = shifts[1] + (PAD - 1 + block * SB)
        for p in range(window):
            for ty in range(3):
                part = deep[first_plane + p, :, pl.ds(first_row + ty, SB), :]
                right[p * depth : (p + 1) * depth, ty * width : (ty + 1) * width] = (
                    part.reshape(depth, width).astype(jnp.bfloat16)
                )
        gram = jnp.dot(left[...], right[...], preferred_element_type=jnp.float32)
        cut = [
            [
                gram[tz * width : (tz + 1) * width, ty * width : (ty + 1) * width]
                for ty in range(3)
            ]
            for tz in range(3)
        ]
        along_z = [cut[t][0] + cut[t][1] + cut[t][2] for t in range(3)]
        along_y = [cut[0][t] + cut[1][t] + cut[2][t] for t in range(3)]
        whole = along_z[0] + along_z[1] + along_z[2]
        far = column - line - shifts[2]
        band = jnp.abs(far) <= 1
        upper = jnp.where(far == 1, whole, 0.0)
        lower = jnp.where(far == -1, whole, 0.0)
        middle = jnp.where(far == 0, whole, 0.0)
        bends = [
            jnp.where(band, 2.0 * g[1] - g[0] - g[2], 0.0) for g in (along_z, along_y)
        ] + [2.0 * middle - lower - upper]
        slopes = [jnp.where(band, g[2] - g[0], 0.0) for g in (along_z, along_y)] + [upper - lower]

        def total(values):
            return jnp.sum(jnp.sum(values, axis=0, keepdims=True), axis=1, keepdims=True) * scale

        sums = [jnp.maximum(total(b), 1.0) for b in bends]
        quality = (sums[0] + sums[1] + sums[2]) / 3.0
        for axis, shift in enumerate(shifts):
            here = lane == block * 3 + axis
            bend_row = jnp.where(here, sums[axis], bend_row)
            slope_row = jnp.where(here, total(slopes[axis]), slope_row)
            centre_row = jnp.where(here, shift.astype(jnp.float32), centre_row)
            quality_row = jnp.where(here, quality, quality_row)
            tether_row = jnp.where(here, settings[0, rows // SB + block], tether_row)

    measured = centre_row + jnp.clip(slope_row / (2.0 * bend_row), -1.0, 1.0)
    gain = quality_row / (quality_row + tether_row)
    other = jnp.where(lane < 3, pltpu.roll(measured, width - 3, 1), pltpu.roll(measured, 3, 1))
    used = lane < 6
    filtered = jnp.where(used, 2.0 * measured + other, 0.0)
    gain = jnp.where(used, gain, 0.0)
    own_out[...] = filtered + pltpu.roll(gain, 8, 1)
    edge_out[...] = pltpu.roll(filtered, 16, 1)


def track_kernel(all_ref, out_ref):
    step, slab, slabs = lax.axis_index("step"), lax.axis_index("gz"), lax.axis_size("gz")
    parity = lax.rem(slab, 2)
    steps = all_ref.shape[0] // 2
    width = all_ref.shape[2]
    lane = lax.broadcasted_iota(jnp.int32, (1, width), 1)
    weight_z = 2.0 + (slab > 0).astype(jnp.float32) + (slab < slabs - 1).astype(jnp.float32)
    weight = jnp.full((1, width), weight_z * 3.0, jnp.float32)
    state = jnp.zeros((1, width), jnp.float32)
    head = all_ref[0:steps, 0, :]
    tail = all_ref[steps : 2 * steps, 0, :]
    mine = jnp.where(parity == 0, head, tail)
    inner = jnp.where(parity == 0, tail, head)
    outer = pltpu.roll(mine, width - 16, 1)
    gain = pltpu.roll(mine, width - 8, 1)
    smooth = (outer + 2.0 * mine + inner) / weight
    keep = 1.0 - gain
    drive = gain * smooth
    for s in range(steps):
        new = keep[s : s + 1] * state + drive[s : s + 1]
        state = jnp.where(s <= step, new, state)
    state = jnp.where(lane < 6, state, 0.0)
    out_ref[0, 0, 0:1, :] = state[:, 0:3]
    out_ref[0, 0, 1:2, :] = pltpu.roll(state, width - 3, 1)[:, 0:3]


def shards(reference_volume, deformed, centres, tether):
    steps, slabs = lax.axis_size("step"), lax.axis_size("gz")
    slab, step = lax.axis_index("gz"), lax.axis_index("step")
    parity = slab & 1
    volume_now = deformed[0]
    planes, channels, rows, width = volume_now.shape
    depth = channels * SB
    window = planes + 2
    blocks = rows // SB
    vmem = pl.BlockSpec(memory_space=pltpu.VMEM)
    anywhere = pl.BlockSpec(memory_space=pl.ANY)
    like = jax.ShapeDtypeStruct

    inside = [(i, i ^ 1) for i in range(slabs)]
    outside = [(i, i + 1) for i in range(1, slabs - 1, 2)]
    outside = outside + [(j, i) for i, j in outside]
    far = planes - HALO
    to_inner = lax.dynamic_slice_in_dim(volume_now, (1 - parity) * far, HALO, 0)
    to_outer = lax.dynamic_slice_in_dim(volume_now, parity * far, HALO, 0)
    copies = jnp.broadcast_to(reference_volume[None], (steps,) + reference_volume.shape)
    outer = lax.ppermute(to_outer, "gz", outside)
    inner = lax.ppermute(to_inner, "gz", inside)
    gathered = lax.all_to_all(copies, "step", split_axis=0, concat_axis=0, tiled=True)
    whole_ref = gathered.transpose(1, 2, 0, 3, 4).reshape(planes, channels, rows, width)

    settings = jnp.concatenate([centres[0, 0].astype(jnp.float32), tether[0]])[None]
    own, edge = pl.pallas_call(
        fit_kernel,
        out_shape=[like((1, width), jnp.float32)] * 2,
        in_specs=[anywhere] + [vmem] * 4,
        out_specs=[vmem] * 2,
        scratch_shapes=[
            pltpu.VMEM((planes + 2 * HALO, channels, rows + 2 * PAD, width), jnp.float32),
            pltpu.VMEM((3 * width, window * depth), jnp.bfloat16),
            pltpu.VMEM((window * depth, 3 * width), jnp.bfloat16),
            pltpu.SMEM((1, 2 * blocks), jnp.float32),
            pltpu.SemaphoreType.DMA,
        ],
        compiler_params=pltpu.CompilerParams(vmem_limit_bytes=40 * MIB),
        name="fit",
    )(settings, whole_ref, volume_now, inner, outer)

    edge = lax.ppermute(edge, "gz", outside)
    row = (own + edge)[None]
    group = 2 * steps
    groups = [[group * i + j for j in range(group)] for i in range(slabs // 2)]
    everyone = lax.all_to_all(
        jnp.broadcast_to(row, (group, 1, width)),
        ("gz", "step"), split_axis=0, concat_axis=0, tiled=True, axis_index_groups=groups,
    )
    return pl.pallas_call(
        track_kernel,
        out_shape=like((1, 1, blocks, 3), jnp.float32),
        in_specs=[vmem],
        out_specs=vmem,
        compiler_params=pltpu.CompilerParams(vmem_limit_bytes=2 * MIB),
        name="track",
    )(everyone)


def solution(mesh):
    placed = (
        P("gz", None, "step", None),
        P("step", "gz", None, None, None),
        P("step", "gz", None),
        P("gz", None),
    )
    return jax.shard_map(
        shards, mesh=mesh, in_specs=placed, out_specs=P("step", "gz", None, None), check_vma=False
    )
```

time: 57.9 us -> 54.4 us (0.940)
  blocking collectives: 0 us -> 10.1 us
  waiting for transfers between devices: 29.9 us -> 22.1 us
  starting transfers between devices: 16.5 us -> 13.2 us
  local copies, waits for them, and re-layouts: 5.48 us -> 4.25 us
  Pallas kernels: 5.05 us -> 4.34 us
    all_to_all x0 -> x1, blocking collectives: none -> 10.1 us  [shards(): lax.all_to_all(jnp.broadcast_to(row, (group, 1, width)), ('gz', 'step'),...]
    all_to_all x1 -> x0, waiting for transfers between devices: 6.89 us -> none  [shards(): lax.all_to_all(jnp.broadcast_to(row, (group, 1, width)), ('gz', 'step'),...]
    all_to_all x1 -> x0, starting transfers between devices: 3.43 us -> none  [shards(): lax.all_to_all(jnp.broadcast_to(row, (group, 1, width)), ('gz', 'step'),...]
    all_to_all x1, waiting for transfers between devices: 18 us -> 17.1 us  [shards(): lax.all_to_all(copies, 'step', split_axis=0, concat_axis=0, tiled=True)]
    pallas_call x2, Pallas kernels: 5.05 us -> 4.34 us  [the longest x1 3.6 us: shards(): pl.pallas_call(fit_kernel, out_shape=[like((1, width), jnp.float32)] * 2,...]
    unnamed x8 -> x6, local copies, waits for them, and re-layouts: 1.26 us -> 0.66 us
    another operation x1 -> x0, other arithmetic: 0.59 us -> none  [shards(): place = jnp.stack([step, slab, jnp.int32(slabs)]).astype(jnp.int32)]
    broadcast_in_dim x1, local copies, waits for them, and re-layouts: 0.6 us -> 0.01 us  [shards(): jnp.broadcast_to(row, (group, 1, width))]
  transfers between devices with their start and end apart: 5 -> 4, of which waited for: 3 -> 2; matrix products, arithmetic and copies ran while one was open for 3% -> 2% of each run, Pallas kernels for 0% -> 0%
where the time goes in v2:
time: 54.4 us; the launch traced here: 54.2 us
  waiting for transfers between devices  22.1 us (41%)
  starting transfers between devices  13.2 us (24%)
  blocking collectives  10.1 us (19%)
  Pallas kernels  4.34 us (8%)
  local copies, waits for them, and re-layouts  4.25 us (8%)
    all_to_all x1, waiting for transfers between devices, shards(): lax.all_to_all(copies, 'step', split_axis=0, concat_axis=0, tiled=True)  17.1 us
    all_to_all x1, blocking collectives, shards(): lax.all_to_all(jnp.broadcast_to(row, (group, 1, width)), ('gz', 'step'),...  10.1 us
    all_to_all x1, starting transfers between devices, shards(): lax.all_to_all(copies, 'step', split_axis=0, concat_axis=0, tiled=True)  7.06 us
    ppermute x1, waiting for transfers between devices, shards(): edge = lax.ppermute(edge, 'gz', outside)  5.04 us
    pallas_call x1, Pallas kernels, shards(): pl.pallas_call(fit_kernel, out_shape=[like((1, width), jnp.float32)] * 2,...  3.6 us
    broadcast_in_dim x1, local copies, waits for them, and re-layouts, shards(): jnp.broadcast_to(reference_volume[None], (steps,) + reference_volume.shape)  2.37 us
    ppermute x1, starting transfers between devices, shards(): outer = lax.ppermute(to_outer, 'gz', outside)  2.15 us
    ppermute x1, starting transfers between devices, shards(): inner = lax.ppermute(to_inner, 'gz', inside)  2.04 us
  transfers between devices with their start and end apart: 4, of which 2 were waited for; matrix products, arithmetic and copies ran while one was open for 2% of the time, Pallas kernels for 0%

profile of v2, /device:TPU:128, one launch (start us, length us, event | category | flops | bytes accessed | tf_op | source)
XLA Modules:
  0.0 54.2 jit_solution(11690893580272137108)
XLA Ops:
  0.0 2.4 %broadcast_in_dim.18 = bf16[8,8,16,4,128]{4,3,2,1,0:T(4,128)(2,1)} broadcast(bf16[8,16,4,128]{3,2,1,0:T(4,128)(2,1)} %param.4), dimensions={1,2,3,4} | broadcast | bytes 1179648 | tf_op jit(solution)/shard_map/broadcast_in_dim | solution.py:166
  2.4 0.0 copy-start
  2.4 7.1 %all-to-all-start = ((bf16[8,8,16,4,128]{4,3,2,1,0:T(4,128)(2,1)}), bf16[8,8,16,4,128]{4,3,2,1,0:T(4,128)(2,1)S(1)}, u32[]{:S(2)}, u32[]{:S(2)}) async-start(bf16[8,8,16,4,128]{4,3,2,1,0:T(4,128)(2,1)} %broadcast_in_dim.18), calls=%async_computation | async-start | bytes 2097152 | tf_op jit(solution)/shard_map/all_to_all | solution.py:169
  9.4 0.0 copy-done
  9.4 0.8 %dynamic-slice_bitcast_fusion = (bf16[3,16,32,128]{3,2,1,0:T(8,128)(2,1)S(1)}, bf16[3,16,32,128]{3,2,1,0:T(8,128)(2,1)}) fusion(bf16[1,8,16,32,128]{4,3,2,1,0:T(8,128)(2,1)S(1)} %copy-done, s32[]{:T(128)S(6)} %select_n.7, s32[]{:T(128)S(6)} %select_n.6), kind=kLoop, calls=%fused_computation | loop fusion | bytes 1572872 | tf_op jit(solution)/shard_map/dynamic_slice | solution.py:165
  10.3 0.0 copy-start.1
  10.3 2.0 %collective-permute-start = (bf16[3,16,32,128]{3,2,1,0:T(8,128)(2,1)}, bf16[3,16,32,128]{3,2,1,0:T(8,128)(2,1)S(1)}, u32[]{:S(2)}, u32[]{:S(2)}) collective-permute-start(bf16[3,16,32,128]{3,2,1,0:T(8,128)(2,1)} %get-tuple-element.10), channel_id=1, source_target_pairs={{0,8},{8,0},{16,24},{24,16},{32,40},{40,32},{48,56},{56,48},{64,72... | collective-permute-start | bytes 1179656 | tf_op jit(solution)/shard_map/ppermute | solution.py:168
  12.3 2.1 %collective-permute-start.1 = (bf16[3,16,32,128]{3,2,1,0:T(8,128)(2,1)S(1)}, bf16[3,16,32,128]{3,2,1,0:T(8,128)(2,1)S(1)}, u32[]{:S(2)}, u32[]{:S(2)}) collective-permute-start(bf16[3,16,32,128]{3,2,1,0:T(8,128)(2,1)S(1)} %get-tuple-element.9), channel_id=1, source_target_pairs={{8,16},{24,32},{40,48},{56,64},{72,80},{88,96},{104,112},{120,128}... | collective-permute-start | bytes 1179656 | tf_op jit(solution)/shard_map/ppermute | solution.py:167
  14.5 0.0 copy-done.1
  14.5 0.0 copy-start.2
  14.5 0.6 %copy-done.2 = f32[1,2]{1,0:T(1,128)S(1)} copy-done((f32[1,2]{1,0:T(1,128)S(1)}, f32[1,2]{1,0:T(1,128)}, u32[]{:S(2)}) %copy-start.2) | copy-done | bytes 32
  15.2 0.1 maximum_bitcast_fusion.settings_hbm
  15.2 17.1 %all-to-all-done = bf16[8,8,16,4,128]{4,3,2,1,0:T(4,128)(2,1)S(1)} async-done(((bf16[8,8,16,4,128]{4,3,2,1,0:T(4,128)(2,1)}), bf16[8,8,16,4,128]{4,3,2,1,0:T(4,128)(2,1)S(1)}, u32[]{:S(2)}, u32[]{:S(2)}) %all-to-all-start) | async-done | bytes 1048608 | tf_op jit(solution)/shard_map/all_to_all | solution.py:169
  32.3 0.4 copy.5
  32.7 0.0 collective-permute-done.inner_ref
  32.7 0.0 collective-permute-done.1.outer_ref
  32.7 3.6 %fit.1 = (f32[1,128]{1,0:T(1,128)S(1)}, f32[1,128]{1,0:T(1,128)S(1)}) custom-call(f32[1,4]{1,0:T(1,128)S(1)} %maximum_bitcast_fusion.settings_hbm, bf16[8,16,32,128]{3,2,1,0:T(8,128)(2,1)S(1)} %bitcast.14, bf16[8,16,32,128]{3,2,1,0:T(8,128)(2,1)S(1)} %bitcast.15, bf16[3,16,32,128]{3,2,1,0:T(8,128)(2,1)S(1)} %collective-permute-done.inner_ref, ...), custom_call_target="tpu_custom_call" | custom-call | tf_op jit(solution)/shard_map/fit/pallas_call | solution.py:173
  36.3 1.9 %collective-permute-start.2 = (f32[1,128]{1,0:T(1,128)S(1)}, f32[1,128]{1,0:T(1,128)S(1)}, u32[]{:S(2)}, u32[]{:S(2)}) collective-permute-start(f32[1,128]{1,0:T(1,128)S(1)} %get-tuple-element.8), channel_id=1, source_target_pairs={{8,16},{24,32},{40,48},{56,64},{72,80},{88,96},{104,112},{120,128}... | collective-permute-start | bytes 1544 | tf_op jit(solution)/shard_map/ppermute | solution.py:189
  38.3 5.0 %collective-permute-done.2 = f32[1,128]{1,0:T(1,128)S(1)} collective-permute-done((f32[1,128]{1,0:T(1,128)S(1)}, f32[1,128]{1,0:T(1,128)S(1)}, u32[]{:S(2)}, u32[]{:S(2)}) %collective-permute-start.2) | collective-permute-done | bytes 544 | tf_op jit(solution)/shard_map/ppermute | solution.py:189
  43.3 10.1 %all_to_all.10.all_ref = f32[16,1,128]{2,1,0:T(1,128)S(1)} all-to-all(f32[16,1,128]{2,1,0:T(1,128)S(1)} %broadcast_in_dim.20), channel_id=1, replica_groups={{0,1,2,3,4,5,6,7,8,9,10,11,12,13,14,15},{16,17,18,19,20,21,22,23,24,25,..., dimensions={0} | all-to-all | bytes 16384 | tf_op jit(solution)/shard_map/all_to_all | solution.py:193
  53.4 0.7 %track.1 = f32[1,1,2,3]{3,2,1,0:T(2,128)} custom-call(f32[16,1,128]{2,1,0:T(1,128)S(1)} %all_to_all.10.all_ref), custom_call_target="tpu_custom_call" | custom-call | tf_op jit(solution)/shard_map/track/pallas_call | solution.py:197
  (3 shorter events, 0.0 us)
Async XLA Ops:
  2.4 7.1 %copy-start = (bf16[1,8,16,32,128]{4,3,2,1,0:T(8,128)(2,1)S(1)}, bf16[1,8,16,32,128]{4,3,2,1,0:T(8,128)(2,1)}, u32[]{:S(2)}) copy-start(bf16[1,8,16,32,128]{4,3,2,1,0:T(8,128)(2,1)} %param.5) | copy-start | bytes 3145732
  2.4 29.9 %all-to-all-start = ((bf16[8,8,16,4,128]{4,3,2,1,0:T(4,128)(2,1)}), bf16[8,8,16,4,128]{4,3,2,1,0:T(4,128)(2,1)S(1)}, u32[]{:S(2)}, u32[]{:S(2)}) async-start(bf16[8,8,16,4,128]{4,3,2,1,0:T(4,128)(2,1)} %broadcast_in_dim.18), calls=%async_computation | async-start | bytes 2097152 | tf_op jit(solution)/shard_map/all_to_all | solution.py:169
  10.3 4.2 %copy-start.1 = (s32[1,1,2]{2,1,0:T(1,128)S(1)}, s32[1,1,2]{2,1,0:T(1,128)}, u32[]{:S(2)}) copy-start(s32[1,1,2]{2,1,0:T(1,128)} %param.6) | copy-start | bytes 28
  10.3 22.5 %collective-permute-start = (bf16[3,16,32,128]{3,2,1,0:T(8,128)(2,1)}, bf16[3,16,32,128]{3,2,1,0:T(8,128)(2,1)S(1)}, u32[]{:S(2)}, u32[]{:S(2)}) collective-permute-start(bf16[3,16,32,128]{3,2,1,0:T(8,128)(2,1)} %get-tuple-element.10), channel_id=1, source_target_pairs={{0,8},{8,0},{16,24},{24,16},{32,40},{40,32},{48,56},{56,48},{64,72... | collective-permute-start | bytes 1179656 | tf_op jit(solution)/shard_map/ppermute | solution.py:168
  12.3 20.4 %collective-permute-start.1 = (bf16[3,16,32,128]{3,2,1,0:T(8,128)(2,1)S(1)}, bf16[3,16,32,128]{3,2,1,0:T(8,128)(2,1)S(1)}, u32[]{:S(2)}, u32[]{:S(2)}) collective-permute-start(bf16[3,16,32,128]{3,2,1,0:T(8,128)(2,1)S(1)} %get-tuple-element.9), channel_id=1, source_target_pairs={{8,16},{24,32},{40,48},{56,64},{72,80},{88,96},{104,112},{120,128}... | collective-permute-start | bytes 1179656 | tf_op jit(solution)/shard_map/ppermute | solution.py:167
  14.5 0.7 %copy-start.2 = (f32[1,2]{1,0:T(1,128)S(1)}, f32[1,2]{1,0:T(1,128)}, u32[]{:S(2)}) copy-start(f32[1,2]{1,0:T(1,128)} %param.7) | copy-start | bytes 28
  36.3 7.0 %collective-permute-start.2 = (f32[1,128]{1,0:T(1,128)S(1)}, f32[1,128]{1,0:T(1,128)S(1)}, u32[]{:S(2)}, u32[]{:S(2)}) collective-permute-start(f32[1,128]{1,0:T(1,128)S(1)} %get-tuple-element.8), channel_id=1, source_target_pairs={{8,16},{24,32},{40,48},{56,64},{72,80},{88,96},{104,112},{120,128}... | collective-permute-start | bytes 1544 | tf_op jit(solution)/shard_map/ppermute | solution.py:189

commit v3 on v2

--- a/solution.py
+++ b/solution.py
@@ -23,7 +23,7 @@
 
 def fit_kernel(
     settings_hbm, r_ref, d_ref, inner_ref, outer_ref,
-    own_out, edge_out, deep, left, right, settings, arrived
+    own_out, edge_out, deep, left_0, left_1, right_0, right_1, settings, arrived
 ):
     planes, channels, rows, width = r_ref.shape
     depth = channels * SB
@@ -43,15 +43,12 @@
     for tz in range(3):
         for p in range(window):
             if p < tz or p >= tz + planes:
-                left[tz * width : (tz + 1) * width, p * depth : (p + 1) * depth] = empty
-    zeros = jnp.zeros((channels, PAD, width), jnp.float32)
+                for left in (left_0, left_1):
+                    left[tz * width : (tz + 1) * width, p * depth : (p + 1) * depth] = empty
     fetch.wait()
     parity = lax.rem(lax.axis_index("gz"), 2)
     inner_at = (1 - parity) * (planes + HALO)
     outer_at = parity * (planes + HALO)
-    for z in range(planes + 2 * HALO):
-        deep[z, :, 0:PAD, :] = zeros
-        deep[z, :, PAD + rows : 2 * PAD + rows, :] = zeros
     for z in range(HALO):
         deep[inner_at + z, :, PAD : PAD + rows, :] = inner_ref[z].astype(jnp.float32)
         deep[outer_at + z, :, PAD : PAD + rows, :] = outer_ref[z].astype(jnp.float32)
@@ -59,18 +56,25 @@
         deep[z + HALO, :, PAD : PAD + rows, :] = d_ref[z].astype(jnp.float32)
 
     for block in range(rows // SB):
+        left, right = ((left_0, right_0), (left_1, right_1))[block]
         shifts = offsets(settings[0, block].astype(jnp.int32))
         for z in range(planes):
-            plane = r_ref[z, :, block * SB : (block + 1) * SB, :].astype(jnp.float32)
-            turned = plane.reshape(depth, width).T.astype(jnp.bfloat16)
+            plane = r_ref[z, :, block * SB : (block + 1) * SB, :]
+            turned = plane.reshape(depth, width).T
             for tz in range(3):
                 p = z + tz
                 left[tz * width : (tz + 1) * width, p * depth : (p + 1) * depth] = turned
         first_plane = shifts[0] + (HALO - 1)
         first_row = shifts[1] + (PAD - 1 + block * SB)
+        height = lax.broadcasted_iota(jnp.int32, (1, SB, width), 1)
+        inside = []
+        for ty in range(3):
+            row = height + (first_row + ty - PAD)
+            inside.append((row >= 0) & (row < rows))
         for p in range(window):
             for ty in range(3):
                 part = deep[first_plane + p, :, pl.ds(first_row + ty, SB), :]
+                part = jnp.where(inside[ty], part, 0.0)
                 right[p * depth : (p + 1) * depth, ty * width : (ty + 1) * width] = (
                     part.reshape(depth, width).astype(jnp.bfloat16)
                 )
@@ -177,8 +181,8 @@
         out_specs=[vmem] * 2,
         scratch_shapes=[
             pltpu.VMEM((planes + 2 * HALO, channels, rows + 2 * PAD, width), jnp.float32),
-            pltpu.VMEM((3 * width, window * depth), jnp.bfloat16),
-            pltpu.VMEM((window * depth, 3 * width), jnp.bfloat16),
+            *([pltpu.VMEM((3 * width, window * depth), jnp.bfloat16)] * blocks),
+            *([pltpu.VMEM((window * depth, 3 * width), jnp.bfloat16)] * blocks),
             pltpu.SMEM((1, 2 * blocks), jnp.float32),
             pltpu.SemaphoreType.DMA,
         ],

time: 54.4 us -> 54.2 us (level)
  no operation moved by 1% of the time
where the time goes in v3:
time: 54.2 us; the launch traced here: 54 us
  waiting for transfers between devices  22.1 us (41%)
  starting transfers between devices  13.2 us (24%)
  blocking collectives  10.1 us (19%)
  local copies, waits for them, and re-layouts  4.25 us (8%)
  Pallas kernels  4.13 us (8%)
    all_to_all x1, waiting for transfers between devices, shards(): lax.all_to_all(copies, 'step', split_axis=0, concat_axis=0, tiled=True)  17.1 us
    all_to_all x1, blocking collectives, shards(): lax.all_to_all(jnp.broadcast_to(row, (group, 1, width)), ('gz', 'step'),...  10.1 us
    all_to_all x1, starting transfers between devices, shards(): lax.all_to_all(copies, 'step', split_axis=0, concat_axis=0, tiled=True)  7.06 us
    ppermute x1, waiting for transfers between devices, shards(): edge = lax.ppermute(edge, 'gz', outside)  5.04 us
    pallas_call x1, Pallas kernels, shards(): pl.pallas_call(fit_kernel, out_shape=[like((1, width), jnp.float32)] * 2,...  3.39 us
    broadcast_in_dim x1, local copies, waits for them, and re-layouts, shards(): jnp.broadcast_to(reference_volume[None], (steps,) + reference_volume.shape)  2.37 us
    ppermute x1, starting transfers between devices, shards(): outer = lax.ppermute(to_outer, 'gz', outside)  2.15 us
    ppermute x1, starting transfers between devices, shards(): inner = lax.ppermute(to_inner, 'gz', inside)  2.04 us
  transfers between devices with their start and end apart: 4, of which 2 were waited for; matrix products, arithmetic and copies ran while one was open for 2% of the time, Pallas kernels for 0%

profile of v3, /device:TPU:128, one launch (start us, length us, event | category | flops | bytes accessed | tf_op | source)
XLA Modules:
  0.0 54.0 jit_solution(1194686439317075742)
XLA Ops:
  0.0 2.4 %broadcast_in_dim.18 = bf16[8,8,16,4,128]{4,3,2,1,0:T(4,128)(2,1)} broadcast(bf16[8,16,4,128]{3,2,1,0:T(4,128)(2,1)} %param.4), dimensions={1,2,3,4} | broadcast | bytes 1179648 | tf_op jit(solution)/shard_map/broadcast_in_dim | solution.py:170
  2.4 0.0 copy-start
  2.4 7.1 %all-to-all-start = ((bf16[8,8,16,4,128]{4,3,2,1,0:T(4,128)(2,1)}), bf16[8,8,16,4,128]{4,3,2,1,0:T(4,128)(2,1)S(1)}, u32[]{:S(2)}, u32[]{:S(2)}) async-start(bf16[8,8,16,4,128]{4,3,2,1,0:T(4,128)(2,1)} %broadcast_in_dim.18), calls=%async_computation | async-start | bytes 2097152 | tf_op jit(solution)/shard_map/all_to_all | solution.py:173
  9.4 0.0 copy-done
  9.4 0.8 %dynamic-slice_bitcast_fusion = (bf16[3,16,32,128]{3,2,1,0:T(8,128)(2,1)S(1)}, bf16[3,16,32,128]{3,2,1,0:T(8,128)(2,1)}) fusion(bf16[1,8,16,32,128]{4,3,2,1,0:T(8,128)(2,1)S(1)} %copy-done, s32[]{:T(128)S(6)} %select_n.7, s32[]{:T(128)S(6)} %select_n.6), kind=kLoop, calls=%fused_computation | loop fusion | bytes 1572872 | tf_op jit(solution)/shard_map/dynamic_slice | solution.py:169
  10.3 0.0 copy-start.1
  10.3 2.0 %collective-permute-start = (bf16[3,16,32,128]{3,2,1,0:T(8,128)(2,1)}, bf16[3,16,32,128]{3,2,1,0:T(8,128)(2,1)S(1)}, u32[]{:S(2)}, u32[]{:S(2)}) collective-permute-start(bf16[3,16,32,128]{3,2,1,0:T(8,128)(2,1)} %get-tuple-element.10), channel_id=1, source_target_pairs={{0,8},{8,0},{16,24},{24,16},{32,40},{40,32},{48,56},{56,48},{64,72... | collective-permute-start | bytes 1179656 | tf_op jit(solution)/shard_map/ppermute | solution.py:172
  12.3 2.1 %collective-permute-start.1 = (bf16[3,16,32,128]{3,2,1,0:T(8,128)(2,1)S(1)}, bf16[3,16,32,128]{3,2,1,0:T(8,128)(2,1)S(1)}, u32[]{:S(2)}, u32[]{:S(2)}) collective-permute-start(bf16[3,16,32,128]{3,2,1,0:T(8,128)(2,1)S(1)} %get-tuple-element.9), channel_id=1, source_target_pairs={{8,16},{24,32},{40,48},{56,64},{72,80},{88,96},{104,112},{120,128}... | collective-permute-start | bytes 1179656 | tf_op jit(solution)/shard_map/ppermute | solution.py:171
  14.5 0.0 copy-done.1
  14.5 0.0 copy-start.2
  14.5 0.6 %copy-done.2 = f32[1,2]{1,0:T(1,128)S(1)} copy-done((f32[1,2]{1,0:T(1,128)S(1)}, f32[1,2]{1,0:T(1,128)}, u32[]{:S(2)}) %copy-start.2) | copy-done | bytes 32
  15.2 0.1 maximum_bitcast_fusion.settings_hbm
  15.2 17.1 %all-to-all-done = bf16[8,8,16,4,128]{4,3,2,1,0:T(4,128)(2,1)S(1)} async-done(((bf16[8,8,16,4,128]{4,3,2,1,0:T(4,128)(2,1)}), bf16[8,8,16,4,128]{4,3,2,1,0:T(4,128)(2,1)S(1)}, u32[]{:S(2)}, u32[]{:S(2)}) %all-to-all-start) | async-done | bytes 1048608 | tf_op jit(solution)/shard_map/all_to_all | solution.py:173
  32.3 0.4 copy.5
  32.7 0.0 collective-permute-done.inner_ref
  32.7 0.0 collective-permute-done.1.outer_ref
  32.7 3.4 %fit.1 = (f32[1,128]{1,0:T(1,128)S(1)}, f32[1,128]{1,0:T(1,128)S(1)}) custom-call(f32[1,4]{1,0:T(1,128)S(1)} %maximum_bitcast_fusion.settings_hbm, bf16[8,16,32,128]{3,2,1,0:T(8,128)(2,1)S(1)} %bitcast.14, bf16[8,16,32,128]{3,2,1,0:T(8,128)(2,1)S(1)} %bitcast.15, bf16[3,16,32,128]{3,2,1,0:T(8,128)(2,1)S(1)} %collective-permute-done.inner_ref, ...), custom_call_target="tpu_custom_call" | custom-call | tf_op jit(solution)/shard_map/fit/pallas_call | solution.py:177
  36.1 1.9 %collective-permute-start.2 = (f32[1,128]{1,0:T(1,128)S(1)}, f32[1,128]{1,0:T(1,128)S(1)}, u32[]{:S(2)}, u32[]{:S(2)}) collective-permute-start(f32[1,128]{1,0:T(1,128)S(1)} %get-tuple-element.8), channel_id=1, source_target_pairs={{8,16},{24,32},{40,48},{56,64},{72,80},{88,96},{104,112},{120,128}... | collective-permute-start | bytes 1544 | tf_op jit(solution)/shard_map/ppermute | solution.py:193
  38.1 5.0 %collective-permute-done.2 = f32[1,128]{1,0:T(1,128)S(1)} collective-permute-done((f32[1,128]{1,0:T(1,128)S(1)}, f32[1,128]{1,0:T(1,128)S(1)}, u32[]{:S(2)}, u32[]{:S(2)}) %collective-permute-start.2) | collective-permute-done | bytes 544 | tf_op jit(solution)/shard_map/ppermute | solution.py:193
  43.1 10.1 %all_to_all.10.all_ref = f32[16,1,128]{2,1,0:T(1,128)S(1)} all-to-all(f32[16,1,128]{2,1,0:T(1,128)S(1)} %broadcast_in_dim.20), channel_id=1, replica_groups={{0,1,2,3,4,5,6,7,8,9,10,11,12,13,14,15},{16,17,18,19,20,21,22,23,24,25,..., dimensions={0} | all-to-all | bytes 16384 | tf_op jit(solution)/shard_map/all_to_all | solution.py:197
  53.2 0.7 %track.1 = f32[1,1,2,3]{3,2,1,0:T(2,128)} custom-call(f32[16,1,128]{2,1,0:T(1,128)S(1)} %all_to_all.10.all_ref), custom_call_target="tpu_custom_call" | custom-call | tf_op jit(solution)/shard_map/track/pallas_call | solution.py:201
  (3 shorter events, 0.0 us)
Async XLA Ops:
  2.4 7.1 %copy-start = (bf16[1,8,16,32,128]{4,3,2,1,0:T(8,128)(2,1)S(1)}, bf16[1,8,16,32,128]{4,3,2,1,0:T(8,128)(2,1)}, u32[]{:S(2)}) copy-start(bf16[1,8,16,32,128]{4,3,2,1,0:T(8,128)(2,1)} %param.5) | copy-start | bytes 3145732
  2.4 29.9 %all-to-all-start = ((bf16[8,8,16,4,128]{4,3,2,1,0:T(4,128)(2,1)}), bf16[8,8,16,4,128]{4,3,2,1,0:T(4,128)(2,1)S(1)}, u32[]{:S(2)}, u32[]{:S(2)}) async-start(bf16[8,8,16,4,128]{4,3,2,1,0:T(4,128)(2,1)} %broadcast_in_dim.18), calls=%async_computation | async-start | bytes 2097152 | tf_op jit(solution)/shard_map/all_to_all | solution.py:173
  10.3 4.2 %copy-start.1 = (s32[1,1,2]{2,1,0:T(1,128)S(1)}, s32[1,1,2]{2,1,0:T(1,128)}, u32[]{:S(2)}) copy-start(s32[1,1,2]{2,1,0:T(1,128)} %param.6) | copy-start | bytes 28
  10.3 22.5 %collective-permute-start = (bf16[3,16,32,128]{3,2,1,0:T(8,128)(2,1)}, bf16[3,16,32,128]{3,2,1,0:T(8,128)(2,1)S(1)}, u32[]{:S(2)}, u32[]{:S(2)}) collective-permute-start(bf16[3,16,32,128]{3,2,1,0:T(8,128)(2,1)} %get-tuple-element.10), channel_id=1, source_target_pairs={{0,8},{8,0},{16,24},{24,16},{32,40},{40,32},{48,56},{56,48},{64,72... | collective-permute-start | bytes 1179656 | tf_op jit(solution)/shard_map/ppermute | solution.py:172
  12.3 20.4 %collective-permute-start.1 = (bf16[3,16,32,128]{3,2,1,0:T(8,128)(2,1)S(1)}, bf16[3,16,32,128]{3,2,1,0:T(8,128)(2,1)S(1)}, u32[]{:S(2)}, u32[]{:S(2)}) collective-permute-start(bf16[3,16,32,128]{3,2,1,0:T(8,128)(2,1)S(1)} %get-tuple-element.9), channel_id=1, source_target_pairs={{8,16},{24,32},{40,48},{56,64},{72,80},{88,96},{104,112},{120,128}... | collective-permute-start | bytes 1179656 | tf_op jit(solution)/shard_map/ppermute | solution.py:171
  14.5 0.7 %copy-start.2 = (f32[1,2]{1,0:T(1,128)S(1)}, f32[1,2]{1,0:T(1,128)}, u32[]{:S(2)}) copy-start(f32[1,2]{1,0:T(1,128)} %param.7) | copy-start | bytes 28
  36.1 7.0 %collective-permute-start.2 = (f32[1,128]{1,0:T(1,128)S(1)}, f32[1,128]{1,0:T(1,128)S(1)}, u32[]{:S(2)}, u32[]{:S(2)}) collective-permute-start(f32[1,128]{1,0:T(1,128)S(1)} %get-tuple-element.8), channel_id=1, source_target_pairs={{8,16},{24,32},{40,48},{56,64},{72,80},{88,96},{104,112},{120,128}... | collective-permute-start | bytes 1544 | tf_op jit(solution)/shard_map/ppermute | solution.py:193

commit v4 on v2

--- a/solution.py
+++ b/solution.py
@@ -163,7 +163,9 @@
     far = planes - HALO
     to_inner = lax.dynamic_slice_in_dim(volume_now, (1 - parity) * far, HALO, 0)
     to_outer = lax.dynamic_slice_in_dim(volume_now, parity * far, HALO, 0)
-    copies = jnp.broadcast_to(reference_volume[None], (steps,) + reference_volume.shape)
+    flat = reference_volume.reshape(-1, width)
+    copies = lax.optimization_barrier(jnp.broadcast_to(flat[None], (steps,) + flat.shape))
+    copies = copies.reshape((steps,) + reference_volume.shape)
     outer = lax.ppermute(to_outer, "gz", outside)
     inner = lax.ppermute(to_inner, "gz", inside)
     gathered = lax.all_to_all(copies, "step", split_axis=0, concat_axis=0, tiled=True)

time: 54.4 us -> 54.7 us (level)
    reshape x0 -> x1, local copies, waits for them, and re-layouts: none -> 1.55 us  [shards(): copies = copies.reshape((steps,) + reference_volume.shape)]
    broadcast_in_dim x1, local copies, waits for them, and re-layouts: 2.37 us -> 1.04 us  [shards(): jnp.broadcast_to(flat[None], (steps,) + flat.shape)]
where the time goes in v4:
time: 54.7 us; the launch traced here: 54.4 us
  waiting for transfers between devices  22.1 us (40%)
  starting transfers between devices  13.2 us (24%)
  blocking collectives  10.1 us (18%)
  local copies, waits for them, and re-layouts  4.47 us (8%)
  Pallas kernels  4.35 us (8%)
    all_to_all x1, waiting for transfers between devices, shards(): lax.all_to_all(copies, 'step', split_axis=0, concat_axis=0, tiled=True)  17.1 us
    all_to_all x1, blocking collectives, shards(): lax.all_to_all(jnp.broadcast_to(row, (group, 1, width)), ('gz', 'step'),...  10.1 us
    all_to_all x1, starting transfers between devices, shards(): lax.all_to_all(copies, 'step', split_axis=0, concat_axis=0, tiled=True)  7.06 us
    ppermute x1, waiting for transfers between devices, shards(): edge = lax.ppermute(edge, 'gz', outside)  5.04 us
    pallas_call x1, Pallas kernels, shards(): pl.pallas_call(fit_kernel, out_shape=[like((1, width), jnp.float32)] * 2,...  3.61 us
    ppermute x1, starting transfers between devices, shards(): outer = lax.ppermute(to_outer, 'gz', outside)  2.15 us
    ppermute x1, starting transfers between devices, shards(): inner = lax.ppermute(to_inner, 'gz', inside)  2.04 us
    ppermute x1, starting transfers between devices, shards(): edge = lax.ppermute(edge, 'gz', outside)  1.92 us
  transfers between devices with their start and end apart: 4, of which 2 were waited for; matrix products, arithmetic and copies ran while one was open for 2% of the time, Pallas kernels for 0%

profile of v4, /device:TPU:128, one launch (start us, length us, event | category | flops | bytes accessed | tf_op | source)
XLA Modules:
  0.0 54.4 jit_solution(12913773689796390639)
XLA Ops:
  0.0 1.0 %broadcast_in_dim.20 = bf16[8,512,128]{2,0,1:T(8,128)(2,1)S(1)} broadcast(bf16[512,128]{1,0:T(8,128)(2,1)} %bitcast.20), dimensions={1,2} | broadcast | bytes 1179648 | tf_op jit(solution)/shard_map/broadcast_in_dim | solution.py:167
  1.0 1.6 %copy.6 = bf16[8,8,16,4,128]{4,3,2,1,0:T(4,128)(2,1)} copy(bf16[8,8,16,4,128]{4,0,3,2,1:T(8,128)(2,1)S(1)} %bitcast.19) | data formatting | bytes 2097152 | tf_op jit(solution)/shard_map/reshape | solution.py:168
  2.6 0.0 copy-start
  2.6 7.1 %all-to-all-start = ((bf16[8,8,16,4,128]{4,3,2,1,0:T(4,128)(2,1)}), bf16[8,8,16,4,128]{4,3,2,1,0:T(4,128)(2,1)S(1)}, u32[]{:S(2)}, u32[]{:S(2)}) async-start(bf16[8,8,16,4,128]{4,3,2,1,0:T(4,128)(2,1)} %copy.6), calls=%async_computation | async-start | bytes 2097152 | tf_op jit(solution)/shard_map/all_to_all | solution.py:171
  9.7 0.0 copy-done
  9.7 0.8 %dynamic-slice_bitcast_fusion = (bf16[3,16,32,128]{3,2,1,0:T(8,128)(2,1)S(1)}, bf16[3,16,32,128]{3,2,1,0:T(8,128)(2,1)}) fusion(bf16[1,8,16,32,128]{4,3,2,1,0:T(8,128)(2,1)S(1)} %copy-done, s32[]{:T(128)S(6)} %select_n.7, s32[]{:T(128)S(6)} %select_n.6), kind=kLoop, calls=%fused_computation | loop fusion | bytes 1572872 | tf_op jit(solution)/shard_map/dynamic_slice | solution.py:165
  10.5 0.0 copy-start.1
  10.5 2.0 %collective-permute-start = (bf16[3,16,32,128]{3,2,1,0:T(8,128)(2,1)}, bf16[3,16,32,128]{3,2,1,0:T(8,128)(2,1)S(1)}, u32[]{:S(2)}, u32[]{:S(2)}) collective-permute-start(bf16[3,16,32,128]{3,2,1,0:T(8,128)(2,1)} %get-tuple-element.10), channel_id=1, source_target_pairs={{0,8},{8,0},{16,24},{24,16},{32,40},{40,32},{48,56},{56,48},{64,72... | collective-permute-start | bytes 1179656 | tf_op jit(solution)/shard_map/ppermute | solution.py:170
  12.5 2.1 %collective-permute-start.1 = (bf16[3,16,32,128]{3,2,1,0:T(8,128)(2,1)S(1)}, bf16[3,16,32,128]{3,2,1,0:T(8,128)(2,1)S(1)}, u32[]{:S(2)}, u32[]{:S(2)}) collective-permute-start(bf16[3,16,32,128]{3,2,1,0:T(8,128)(2,1)S(1)} %get-tuple-element.9), channel_id=1, source_target_pairs={{8,16},{24,32},{40,48},{56,64},{72,80},{88,96},{104,112},{120,128}... | collective-permute-start | bytes 1179656 | tf_op jit(solution)/shard_map/ppermute | solution.py:169
  14.7 0.0 copy-done.1
  14.7 0.0 copy-start.2
  14.7 0.6 %copy-done.2 = f32[1,2]{1,0:T(1,128)S(1)} copy-done((f32[1,2]{1,0:T(1,128)S(1)}, f32[1,2]{1,0:T(1,128)}, u32[]{:S(2)}) %copy-start.2) | copy-done | bytes 32
  15.4 0.1 maximum_bitcast_fusion.settings_hbm
  15.4 17.1 %all-to-all-done = bf16[8,8,16,4,128]{4,3,2,1,0:T(4,128)(2,1)S(1)} async-done(((bf16[8,8,16,4,128]{4,3,2,1,0:T(4,128)(2,1)}), bf16[8,8,16,4,128]{4,3,2,1,0:T(4,128)(2,1)S(1)}, u32[]{:S(2)}, u32[]{:S(2)}) %all-to-all-start) | async-done | bytes 1048608 | tf_op jit(solution)/shard_map/all_to_all | solution.py:171
  32.5 0.4 copy.7
  32.9 0.0 collective-permute-done.inner_ref
  33.0 0.0 collective-permute-done.1.outer_ref
  33.0 3.6 %fit.1 = (f32[1,128]{1,0:T(1,128)S(1)}, f32[1,128]{1,0:T(1,128)S(1)}) custom-call(f32[1,4]{1,0:T(1,128)S(1)} %maximum_bitcast_fusion.settings_hbm, bf16[8,16,32,128]{3,2,1,0:T(8,128)(2,1)S(1)} %bitcast.16, bf16[8,16,32,128]{3,2,1,0:T(8,128)(2,1)S(1)} %bitcast.17, bf16[3,16,32,128]{3,2,1,0:T(8,128)(2,1)S(1)} %collective-permute-done.inner_ref, ...), custom_call_target="tpu_custom_call" | custom-call | tf_op jit(solution)/shard_map/fit/pallas_call | solution.py:175
  36.6 1.9 %collective-permute-start.2 = (f32[1,128]{1,0:T(1,128)S(1)}, f32[1,128]{1,0:T(1,128)S(1)}, u32[]{:S(2)}, u32[]{:S(2)}) collective-permute-start(f32[1,128]{1,0:T(1,128)S(1)} %get-tuple-element.8), channel_id=1, source_target_pairs={{8,16},{24,32},{40,48},{56,64},{72,80},{88,96},{104,112},{120,128}... | collective-permute-start | bytes 1544 | tf_op jit(solution)/shard_map/ppermute | solution.py:191
  38.5 5.0 %collective-permute-done.2 = f32[1,128]{1,0:T(1,128)S(1)} collective-permute-done((f32[1,128]{1,0:T(1,128)S(1)}, f32[1,128]{1,0:T(1,128)S(1)}, u32[]{:S(2)}, u32[]{:S(2)}) %collective-permute-start.2) | collective-permute-done | bytes 544 | tf_op jit(solution)/shard_map/ppermute | solution.py:191
  43.6 10.1 %all_to_all.10.all_ref = f32[16,1,128]{2,1,0:T(1,128)S(1)} all-to-all(f32[16,1,128]{2,1,0:T(1,128)S(1)} %broadcast_in_dim.22), channel_id=1, replica_groups={{0,1,2,3,4,5,6,7,8,9,10,11,12,13,14,15},{16,17,18,19,20,21,22,23,24,25,..., dimensions={0} | all-to-all | bytes 16384 | tf_op jit(solution)/shard_map/all_to_all | solution.py:195
  53.7 0.7 %track.1 = f32[1,1,2,3]{3,2,1,0:T(2,128)} custom-call(f32[16,1,128]{2,1,0:T(1,128)S(1)} %all_to_all.10.all_ref), custom_call_target="tpu_custom_call" | custom-call | tf_op jit(solution)/shard_map/track/pallas_call | solution.py:199
  (3 shorter events, 0.0 us)
Async XLA Ops:
  2.6 7.1 %copy-start = (bf16[1,8,16,32,128]{4,3,2,1,0:T(8,128)(2,1)S(1)}, bf16[1,8,16,32,128]{4,3,2,1,0:T(8,128)(2,1)}, u32[]{:S(2)}) copy-start(bf16[1,8,16,32,128]{4,3,2,1,0:T(8,128)(2,1)} %param.5) | copy-start | bytes 3145732
  2.6 29.9 %all-to-all-start = ((bf16[8,8,16,4,128]{4,3,2,1,0:T(4,128)(2,1)}), bf16[8,8,16,4,128]{4,3,2,1,0:T(4,128)(2,1)S(1)}, u32[]{:S(2)}, u32[]{:S(2)}) async-start(bf16[8,8,16,4,128]{4,3,2,1,0:T(4,128)(2,1)} %copy.6), calls=%async_computation | async-start | bytes 2097152 | tf_op jit(solution)/shard_map/all_to_all | solution.py:171
  10.5 4.2 %copy-start.1 = (s32[1,1,2]{2,1,0:T(1,128)S(1)}, s32[1,1,2]{2,1,0:T(1,128)}, u32[]{:S(2)}) copy-start(s32[1,1,2]{2,1,0:T(1,128)} %param.6) | copy-start | bytes 28
  10.5 22.5 %collective-permute-start = (bf16[3,16,32,128]{3,2,1,0:T(8,128)(2,1)}, bf16[3,16,32,128]{3,2,1,0:T(8,128)(2,1)S(1)}, u32[]{:S(2)}, u32[]{:S(2)}) collective-permute-start(bf16[3,16,32,128]{3,2,1,0:T(8,128)(2,1)} %get-tuple-element.10), channel_id=1, source_target_pairs={{0,8},{8,0},{16,24},{24,16},{32,40},{40,32},{48,56},{56,48},{64,72... | collective-permute-start | bytes 1179656 | tf_op jit(solution)/shard_map/ppermute | solution.py:170
  12.5 20.4 %collective-permute-start.1 = (bf16[3,16,32,128]{3,2,1,0:T(8,128)(2,1)S(1)}, bf16[3,16,32,128]{3,2,1,0:T(8,128)(2,1)S(1)}, u32[]{:S(2)}, u32[]{:S(2)}) collective-permute-start(bf16[3,16,32,128]{3,2,1,0:T(8,128)(2,1)S(1)} %get-tuple-element.9), channel_id=1, source_target_pairs={{8,16},{24,32},{40,48},{56,64},{72,80},{88,96},{104,112},{120,128}... | collective-permute-start | bytes 1179656 | tf_op jit(solution)/shard_map/ppermute | solution.py:169
  14.7 0.7 %copy-start.2 = (f32[1,2]{1,0:T(1,128)S(1)}, f32[1,2]{1,0:T(1,128)}, u32[]{:S(2)}) copy-start(f32[1,2]{1,0:T(1,128)} %param.7) | copy-start | bytes 28
  36.6 7.0 %collective-permute-start.2 = (f32[1,128]{1,0:T(1,128)S(1)}, f32[1,128]{1,0:T(1,128)S(1)}, u32[]{:S(2)}, u32[]{:S(2)}) collective-permute-start(f32[1,128]{1,0:T(1,128)S(1)} %get-tuple-element.8), channel_id=1, source_target_pairs={{8,16},{24,32},{40,48},{56,64},{72,80},{88,96},{104,112},{120,128}... | collective-permute-start | bytes 1544 | tf_op jit(solution)/shard_map/ppermute | solution.py:191

commit v5 on v2

--- a/solution.py
+++ b/solution.py
@@ -39,11 +39,6 @@
     centre_row = jnp.zeros((1, width), jnp.float32)
     quality_row = jnp.ones((1, width), jnp.float32)
     tether_row = jnp.ones((1, width), jnp.float32)
-    empty = jnp.zeros((width, depth), jnp.bfloat16)
-    for tz in range(3):
-        for p in range(window):
-            if p < tz or p >= tz + planes:
-                left[tz * width : (tz + 1) * width, p * depth : (p + 1) * depth] = empty
     zeros = jnp.zeros((channels, PAD, width), jnp.float32)
     fetch.wait()
     parity = lax.rem(lax.axis_index("gz"), 2)
@@ -63,9 +58,7 @@
         for z in range(planes):
             plane = r_ref[z, :, block * SB : (block + 1) * SB, :].astype(jnp.float32)
             turned = plane.reshape(depth, width).T.astype(jnp.bfloat16)
-            for tz in range(3):
-                p = z + tz
-                left[tz * width : (tz + 1) * width, p * depth : (p + 1) * depth] = turned
+            left[:, z * depth : (z + 1) * depth] = turned
         first_plane = shifts[0] + (HALO - 1)
         first_row = shifts[1] + (PAD - 1 + block * SB)
         for p in range(window):
@@ -74,14 +67,15 @@
                 right[p * depth : (p + 1) * depth, ty * width : (ty + 1) * width] = (
                     part.reshape(depth, width).astype(jnp.bfloat16)
                 )
-        gram = jnp.dot(left[...], right[...], preferred_element_type=jnp.float32)
-        cut = [
-            [
-                gram[tz * width : (tz + 1) * width, ty * width : (ty + 1) * width]
-                for ty in range(3)
-            ]
+        grams = [
+            jnp.dot(
+                left[...],
+                right[tz * depth : (tz + planes) * depth, :],
+                preferred_element_type=jnp.float32,
+            )
             for tz in range(3)
         ]
+        cut = [[gram[:, ty * width : (ty + 1) * width] for ty in range(3)] for gram in grams]
         along_z = [cut[t][0] + cut[t][1] + cut[t][2] for t in range(3)]
         along_y = [cut[0][t] + cut[1][t] + cut[2][t] for t in range(3)]
         whole = along_z[0] + along_z[1] + along_z[2]
@@ -177,7 +171,7 @@
         out_specs=[vmem] * 2,
         scratch_shapes=[
             pltpu.VMEM((planes + 2 * HALO, channels, rows + 2 * PAD, width), jnp.float32),
-            pltpu.VMEM((3 * width, window * depth), jnp.bfloat16),
+            pltpu.VMEM((width, planes * depth), jnp.bfloat16),
             pltpu.VMEM((window * depth, 3 * width), jnp.bfloat16),
             pltpu.SMEM((1, 2 * blocks), jnp.float32),
             pltpu.SemaphoreType.DMA,

time: 54.4 us -> 54.4 us (level)
  no operation moved by 1% of the time
where the time goes in v5:
time: 54.4 us; the launch traced here: 54.2 us
  waiting for transfers between devices  22.1 us (41%)
  starting transfers between devices  13.2 us (24%)
  blocking collectives  10.1 us (19%)
  Pallas kernels  4.38 us (8%)
  local copies, waits for them, and re-layouts  4.25 us (8%)
    all_to_all x1, waiting for transfers between devices, shards(): lax.all_to_all(copies, 'step', split_axis=0, concat_axis=0, tiled=True)  17.1 us
    all_to_all x1, blocking collectives, shards(): lax.all_to_all(jnp.broadcast_to(row, (group, 1, width)), ('gz', 'step'),...  10.1 us
    all_to_all x1, starting transfers between devices, shards(): lax.all_to_all(copies, 'step', split_axis=0, concat_axis=0, tiled=True)  7.06 us
    ppermute x1, waiting for transfers between devices, shards(): edge = lax.ppermute(edge, 'gz', outside)  5.04 us
    pallas_call x1, Pallas kernels, shards(): pl.pallas_call(fit_kernel, out_shape=[like((1, width), jnp.float32)] * 2,...  3.64 us
    broadcast_in_dim x1, local copies, waits for them, and re-layouts, shards(): jnp.broadcast_to(reference_volume[None], (steps,) + reference_volume.shape)  2.37 us
    ppermute x1, starting transfers between devices, shards(): outer = lax.ppermute(to_outer, 'gz', outside)  2.15 us
    ppermute x1, starting transfers between devices, shards(): inner = lax.ppermute(to_inner, 'gz', inside)  2.04 us
  transfers between devices with their start and end apart: 4, of which 2 were waited for; matrix products, arithmetic and copies ran while one was open for 2% of the time, Pallas kernels for 0%

profile of v5, /device:TPU:128, one launch (start us, length us, event | category | flops | bytes accessed | tf_op | source)
XLA Modules:
  0.0 54.2 jit_solution(9749875949605265201)
XLA Ops:
  0.0 2.4 %broadcast_in_dim.18 = bf16[8,8,16,4,128]{4,3,2,1,0:T(4,128)(2,1)} broadcast(bf16[8,16,4,128]{3,2,1,0:T(4,128)(2,1)} %param.4), dimensions={1,2,3,4} | broadcast | bytes 1179648 | tf_op jit(solution)/shard_map/broadcast_in_dim | solution.py:160
  2.4 0.0 copy-start
  2.4 7.1 %all-to-all-start = ((bf16[8,8,16,4,128]{4,3,2,1,0:T(4,128)(2,1)}), bf16[8,8,16,4,128]{4,3,2,1,0:T(4,128)(2,1)S(1)}, u32[]{:S(2)}, u32[]{:S(2)}) async-start(bf16[8,8,16,4,128]{4,3,2,1,0:T(4,128)(2,1)} %broadcast_in_dim.18), calls=%async_computation | async-start | bytes 2097152 | tf_op jit(solution)/shard_map/all_to_all | solution.py:163
  9.4 0.0 copy-done
  9.4 0.8 %dynamic-slice_bitcast_fusion = (bf16[3,16,32,128]{3,2,1,0:T(8,128)(2,1)S(1)}, bf16[3,16,32,128]{3,2,1,0:T(8,128)(2,1)}) fusion(bf16[1,8,16,32,128]{4,3,2,1,0:T(8,128)(2,1)S(1)} %copy-done, s32[]{:T(128)S(6)} %select_n.7, s32[]{:T(128)S(6)} %select_n.6), kind=kLoop, calls=%fused_computation | loop fusion | bytes 1572872 | tf_op jit(solution)/shard_map/dynamic_slice | solution.py:159
  10.3 0.0 copy-start.1
  10.3 2.0 %collective-permute-start = (bf16[3,16,32,128]{3,2,1,0:T(8,128)(2,1)}, bf16[3,16,32,128]{3,2,1,0:T(8,128)(2,1)S(1)}, u32[]{:S(2)}, u32[]{:S(2)}) collective-permute-start(bf16[3,16,32,128]{3,2,1,0:T(8,128)(2,1)} %get-tuple-element.10), channel_id=1, source_target_pairs={{0,8},{8,0},{16,24},{24,16},{32,40},{40,32},{48,56},{56,48},{64,72... | collective-permute-start | bytes 1179656 | tf_op jit(solution)/shard_map/ppermute | solution.py:162
  12.3 2.1 %collective-permute-start.1 = (bf16[3,16,32,128]{3,2,1,0:T(8,128)(2,1)S(1)}, bf16[3,16,32,128]{3,2,1,0:T(8,128)(2,1)S(1)}, u32[]{:S(2)}, u32[]{:S(2)}) collective-permute-start(bf16[3,16,32,128]{3,2,1,0:T(8,128)(2,1)S(1)} %get-tuple-element.9), channel_id=1, source_target_pairs={{8,16},{24,32},{40,48},{56,64},{72,80},{88,96},{104,112},{120,128}... | collective-permute-start | bytes 1179656 | tf_op jit(solution)/shard_map/ppermute | solution.py:161
  14.5 0.0 copy-done.1
  14.5 0.0 copy-start.2
  14.5 0.6 %copy-done.2 = f32[1,2]{1,0:T(1,128)S(1)} copy-done((f32[1,2]{1,0:T(1,128)S(1)}, f32[1,2]{1,0:T(1,128)}, u32[]{:S(2)}) %copy-start.2) | copy-done | bytes 32
  15.2 0.1 maximum_bitcast_fusion.settings_hbm
  15.2 17.1 %all-to-all-done = bf16[8,8,16,4,128]{4,3,2,1,0:T(4,128)(2,1)S(1)} async-done(((bf16[8,8,16,4,128]{4,3,2,1,0:T(4,128)(2,1)}), bf16[8,8,16,4,128]{4,3,2,1,0:T(4,128)(2,1)S(1)}, u32[]{:S(2)}, u32[]{:S(2)}) %all-to-all-start) | async-done | bytes 1048608 | tf_op jit(solution)/shard_map/all_to_all | solution.py:163
  32.3 0.4 copy.5
  32.7 0.0 collective-permute-done.inner_ref
  32.7 0.0 collective-permute-done.1.outer_ref
  32.7 3.6 %fit.1 = (f32[1,128]{1,0:T(1,128)S(1)}, f32[1,128]{1,0:T(1,128)S(1)}) custom-call(f32[1,4]{1,0:T(1,128)S(1)} %maximum_bitcast_fusion.settings_hbm, bf16[8,16,32,128]{3,2,1,0:T(8,128)(2,1)S(1)} %bitcast.14, bf16[8,16,32,128]{3,2,1,0:T(8,128)(2,1)S(1)} %bitcast.15, bf16[3,16,32,128]{3,2,1,0:T(8,128)(2,1)S(1)} %collective-permute-done.inner_ref, ...), custom_call_target="tpu_custom_call" | custom-call | tf_op jit(solution)/shard_map/fit/pallas_call | solution.py:167
  36.4 1.9 %collective-permute-start.2 = (f32[1,128]{1,0:T(1,128)S(1)}, f32[1,128]{1,0:T(1,128)S(1)}, u32[]{:S(2)}, u32[]{:S(2)}) collective-permute-start(f32[1,128]{1,0:T(1,128)S(1)} %get-tuple-element.8), channel_id=1, source_target_pairs={{8,16},{24,32},{40,48},{56,64},{72,80},{88,96},{104,112},{120,128}... | collective-permute-start | bytes 1544 | tf_op jit(solution)/shard_map/ppermute | solution.py:183
  38.3 5.0 %collective-permute-done.2 = f32[1,128]{1,0:T(1,128)S(1)} collective-permute-done((f32[1,128]{1,0:T(1,128)S(1)}, f32[1,128]{1,0:T(1,128)S(1)}, u32[]{:S(2)}, u32[]{:S(2)}) %collective-permute-start.2) | collective-permute-done | bytes 544 | tf_op jit(solution)/shard_map/ppermute | solution.py:183
  43.4 10.1 %all_to_all.10.all_ref = f32[16,1,128]{2,1,0:T(1,128)S(1)} all-to-all(f32[16,1,128]{2,1,0:T(1,128)S(1)} %broadcast_in_dim.20), channel_id=1, replica_groups={{0,1,2,3,4,5,6,7,8,9,10,11,12,13,14,15},{16,17,18,19,20,21,22,23,24,25,..., dimensions={0} | all-to-all | bytes 16384 | tf_op jit(solution)/shard_map/all_to_all | solution.py:187
  53.5 0.7 %track.1 = f32[1,1,2,3]{3,2,1,0:T(2,128)} custom-call(f32[16,1,128]{2,1,0:T(1,128)S(1)} %all_to_all.10.all_ref), custom_call_target="tpu_custom_call" | custom-call | tf_op jit(solution)/shard_map/track/pallas_call | solution.py:191
  (3 shorter events, 0.0 us)
Async XLA Ops:
  2.4 7.1 %copy-start = (bf16[1,8,16,32,128]{4,3,2,1,0:T(8,128)(2,1)S(1)}, bf16[1,8,16,32,128]{4,3,2,1,0:T(8,128)(2,1)}, u32[]{:S(2)}) copy-start(bf16[1,8,16,32,128]{4,3,2,1,0:T(8,128)(2,1)} %param.5) | copy-start | bytes 3145732
  2.4 29.9 %all-to-all-start = ((bf16[8,8,16,4,128]{4,3,2,1,0:T(4,128)(2,1)}), bf16[8,8,16,4,128]{4,3,2,1,0:T(4,128)(2,1)S(1)}, u32[]{:S(2)}, u32[]{:S(2)}) async-start(bf16[8,8,16,4,128]{4,3,2,1,0:T(4,128)(2,1)} %broadcast_in_dim.18), calls=%async_computation | async-start | bytes 2097152 | tf_op jit(solution)/shard_map/all_to_all | solution.py:163
  10.3 4.2 %copy-start.1 = (s32[1,1,2]{2,1,0:T(1,128)S(1)}, s32[1,1,2]{2,1,0:T(1,128)}, u32[]{:S(2)}) copy-start(s32[1,1,2]{2,1,0:T(1,128)} %param.6) | copy-start | bytes 28
  10.3 22.5 %collective-permute-start = (bf16[3,16,32,128]{3,2,1,0:T(8,128)(2,1)}, bf16[3,16,32,128]{3,2,1,0:T(8,128)(2,1)S(1)}, u32[]{:S(2)}, u32[]{:S(2)}) collective-permute-start(bf16[3,16,32,128]{3,2,1,0:T(8,128)(2,1)} %get-tuple-element.10), channel_id=1, source_target_pairs={{0,8},{8,0},{16,24},{24,16},{32,40},{40,32},{48,56},{56,48},{64,72... | collective-permute-start | bytes 1179656 | tf_op jit(solution)/shard_map/ppermute | solution.py:162
  12.3 20.4 %collective-permute-start.1 = (bf16[3,16,32,128]{3,2,1,0:T(8,128)(2,1)S(1)}, bf16[3,16,32,128]{3,2,1,0:T(8,128)(2,1)S(1)}, u32[]{:S(2)}, u32[]{:S(2)}) collective-permute-start(bf16[3,16,32,128]{3,2,1,0:T(8,128)(2,1)S(1)} %get-tuple-element.9), channel_id=1, source_target_pairs={{8,16},{24,32},{40,48},{56,64},{72,80},{88,96},{104,112},{120,128}... | collective-permute-start | bytes 1179656 | tf_op jit(solution)/shard_map/ppermute | solution.py:161
  14.5 0.7 %copy-start.2 = (f32[1,2]{1,0:T(1,128)S(1)}, f32[1,2]{1,0:T(1,128)}, u32[]{:S(2)}) copy-start(f32[1,2]{1,0:T(1,128)} %param.7) | copy-start | bytes 28
  36.4 7.0 %collective-permute-start.2 = (f32[1,128]{1,0:T(1,128)S(1)}, f32[1,128]{1,0:T(1,128)S(1)}, u32[]{:S(2)}, u32[]{:S(2)}) collective-permute-start(f32[1,128]{1,0:T(1,128)S(1)} %get-tuple-element.8), channel_id=1, source_target_pairs={{8,16},{24,32},{40,48},{56,64},{72,80},{88,96},{104,112},{120,128}... | collective-permute-start | bytes 1544 | tf_op jit(solution)/shard_map/ppermute | solution.py:183
